TPU v7x, 512 devices: a whole 4x8x8 slice. The times are simulated.
512 devices in a mesh: slab: 16 (over y, core), sub: 32 (over z, x).
Axes of the slice: x: 4, y: 8, z: 8, core: 2. Of those that a mesh axis runs over, the one named last changes fastest.
Arguments:
- positions: float32 [3, 8192, 256], P(None, ('slab', 'sub')), may hold values from 0 to 1
- velocities: float32 [3, 8192, 256], P(None, ('slab', 'sub')), may hold values from -6 to 6
- mass: float32 [8192, 256], P(('slab', 'sub')), may hold values from 0.0001953125 to 0.0009765625
- smoothing: float32 [8192, 256], P(('slab', 'sub')), may hold values from 0.08 to 0.15
- energy: float32 [8192, 256], P(('slab', 'sub')), may hold values from 0.2 to 2
- cell_counts: int32 [8192], P(('slab', 'sub')), may hold values from 128 to 256, as said below
- send_cells: int32 [512, 32, 2], P(('slab', 'sub')), may hold values from 0 to 15, as said below
- partners: int32 [8192, 8], P(('slab', 'sub')), may hold values from 0 to 81, as said below
- mig_list: int32 [512, 32, 8], P(('slab', 'sub')), may hold values from 0 to 4095, as said below
- mig_counts: int32 [512, 32], P(('slab', 'sub')), may hold values from 1 to 8, as said below
Outputs:
- density: float32 [8192, 256], P(('slab', 'sub'))
- state: float32 [6, 8192, 256], P(None, ('slab', 'sub'))
- arrivals: float32 [6, 131072], P(None, ('slab', 'sub'))
Inputs may be any that keep to these rules, and one draw needn't show every extreme that they name: `cell_counts`: every cell has at least half of its slots live; the first cell holds 256. `send_cells`: the 2 cells sent to one device are distinct. `partners`: a row is distinct indices; its first is the cell itself (1 plus its index within the device), its second a lower rim cell for the first half of a device's cells and an upper rim cell for the second half. `mig_list`: every entry names a live slot. `mig_counts`: each device sends 8 to some device of its slab, and in each slab one device receives 8 from every sender.
All inputs are finite; a program needn't handle non-finite values.
Results may differ from a plain program's by a relative error of at most 0.0003.
Values sent between devices are 32-bit elements; how exact they have to be, the bound alone decides.
No kernel may reach another device: no remote copies, remote signals or barrier semaphores. Data moves between devices by JAX's collectives and lax.ppermute only.
A program may use at most 64 MiB of HBM per device.

v0:
```python
import math

import jax
import jax.numpy as jnp
from jax import lax
from jax.sharding import PartitionSpec as P

P_SIZE = 256
HB = 1
M = 8


adiabatic = 5.0 / 3.0
time_step = 0.05


def extended(value, sides, width):
    for axis, dim in sides:
        count, length = (lax.axis_size(axis), value.shape[dim])
        up = [(i, (i + 1) % count) for i in range(count)]
        down = [(j, i) for i, j in up]
        last = lax.slice_in_dim(value, length - width, length, axis=dim)
        leading = lax.slice_in_dim(value, 0, width, axis=dim)
        before = lax.ppermute(last, axis, up)
        after = lax.ppermute(leading, axis, down)
        value = jnp.concatenate([before, value, after], axis=dim)
    return value


def separation(own_pos, others):
    apart_x = own_pos[0][:, None] - others[0][None, :]
    apart_y = own_pos[1][:, None] - others[1][None, :]
    apart_z = own_pos[2][:, None] - others[2][None, :]
    radius = jnp.sqrt(apart_x * apart_x + apart_y * apart_y + apart_z * apart_z)
    return (apart_x, apart_y, apart_z, radius)


def pair_density(own_pos, own_width, nearby):
    others = nearby[:3].reshape(3, -1)
    masses = nearby[3].reshape(-1)
    apart_x, apart_y, apart_z, radius = separation(own_pos, others)
    scaled = radius / own_width[:, None]
    inside = 1.0 - 1.5 * scaled * scaled + 0.75 * scaled * scaled * scaled
    remain = jnp.maximum(2.0 - scaled, 0.0)
    kernel = jnp.where(scaled < 1.0, inside, 0.25 * remain * remain * remain)
    return jnp.sum(kernel * masses[None, :], axis=1) / (math.pi * own_width**3)


def pair_force(own_pos, own_width, own_press, nearby):
    others = nearby[:3].reshape(3, -1)
    masses = nearby[3].reshape(-1)
    press = nearby[4].reshape(-1)
    apart_x, apart_y, apart_z, radius = separation(own_pos, others)
    scaled = radius / own_width[:, None]
    remain = jnp.maximum(2.0 - scaled, 0.0)
    slope = jnp.where(
        scaled < 1.0, -3.0 + 2.25 * scaled, -0.75 * remain * remain / jnp.maximum(scaled, 1.0)
    )
    factor = masses[None, :] * (own_press[:, None] + press[None, :]) * slope
    push = jnp.stack(
        [
            jnp.sum(factor * apart_x, axis=1),
            jnp.sum(factor * apart_y, axis=1),
            jnp.sum(factor * apart_z, axis=1),
        ]
    )
    return -push / (math.pi * own_width**5)


def density_cell(items):
    return pair_density(items[0], items[1], items[2])


def force_cell(items):
    return pair_force(items[0], items[1], items[2], items[3])


def on_device(
    positions,
    velocities,
    mass,
    smoothing,
    energy,
    cell_counts,
    send_cells,
    partners,
    mig_list,
    mig_counts,
):
    cells = mass.shape[0]
    peers = lax.axis_size("sub")
    here = lax.axis_index("sub")
    valid = jnp.arange(P_SIZE)[None, :] < cell_counts[:, None]
    mass_live = jnp.where(valid, mass, 0.0)
    block = jnp.concatenate([positions, mass_live[None]], axis=0)
    rimmed = extended(block, (("slab", 1),), HB)
    every, lists = (
        lax.all_gather(block, "sub", axis=1, tiled=True),
        lax.all_gather(send_cells, "sub", axis=0, tiled=True),
    )
    wanted = (jnp.arange(peers)[:, None] * cells + lists[:, here, :]).reshape(-1)
    proxies = every[:, wanted, :]
    table = jnp.concatenate([rimmed, proxies], axis=1)
    nearby = jnp.moveaxis(table[:, partners, :], 1, 0)
    own_pos = jnp.moveaxis(positions, 1, 0)
    density = lax.map(density_cell, (own_pos, smoothing, nearby))
    pressure = jnp.where(valid, (adiabatic - 1.0) * energy / jnp.where(valid, density, 1.0), 0.0)
    press_block = pressure[None]
    press_rimmed = extended(press_block, (("slab", 1),), HB)
    press_every = lax.all_gather(press_block, "sub", axis=1, tiled=True)
    press_proxies = press_every[:, wanted, :]
    press_table = jnp.concatenate([press_rimmed, press_proxies], axis=1)
    full = jnp.concatenate([table, press_table], axis=0)
    nearby_all = jnp.moveaxis(full[:, partners, :], 1, 0)
    push = lax.map(force_cell, (own_pos, smoothing, pressure, nearby_all))
    velocity = velocities + time_step * jnp.moveaxis(push, 0, 1)
    place = positions + time_step * velocity
    state = jnp.where(valid[None], jnp.concatenate([place, velocity], axis=0), 0.0)
    flat = state.reshape(6, cells * P_SIZE)
    leaving = flat[:, mig_list[0].reshape(-1)].reshape(6, peers, M)
    arrived, counts = (
        lax.all_to_all(leaving, "sub", split_axis=1, concat_axis=1, tiled=True),
        lax.all_to_all(mig_counts, "sub", split_axis=1, concat_axis=1, tiled=True),
    )
    keep = jnp.arange(M)[None, :] < counts[0][:, None]
    arrivals = jnp.where(keep[None], arrived, 0.0).reshape(6, peers * M)
    return (jnp.where(valid, density, 0.0), state, arrivals)


def solution(mesh):
    return jax.shard_map(
        on_device,
        mesh=mesh,
        in_specs=(
            P(None, ("slab", "sub"), None),
            P(None, ("slab", "sub"), None),
            P(("slab", "sub"), None),
            P(("slab", "sub"), None),
            P(("slab", "sub"), None),
            P(("slab", "sub")),
            P(("slab", "sub"), None, None),
            P(("slab", "sub"), None),
            P(("slab", "sub"), None, None),
            P(("slab", "sub"), None),
        ),
        out_specs=(
            P(("slab", "sub"), None),
            P(None, ("slab", "sub"), None),
            P(None, ("slab", "sub")),
        ),
        check_vma=False,
    )
```

profile of v0, /device:TPU:32, one launch (start us, length us, event | category | flops | bytes accessed | tf_op | source)
XLA Modules:
  0.0 309.6 jit_solution(12017114337561359657)
XLA Ops:
  9.6 2.9 collective-permute-start.1
  13.9 13.2 %all-to-all-start = ((s32[1,32,1]{2,0,1:T(1,128)}), s32[1,32,1]{2,0,1:T(1,128)S(1)}, u32[]{:S(2)}, u32[]{:S(2)}) async-start(s32[1,32,1]{2,0,1:T(1,128)} %copy.89), calls=%async_computation | async-start | bytes 32768 | tf_op jit(solution)/shard_map/all_to_all | solution.py:123
  27.1 43.6 %all_gather.10 = s32[32,32,2]{1,2,0:T(2,128)S(1)} all-gather(s32[1,32,2]{1,2,0:T(2,128)} %param.20), channel_id=1, replica_groups=mesh['slab'=16,'sub'=32] {'sub'}, dimensions={0}, use_global_device_ids=true | all-gather | bytes 8448 | tf_op jit(solution)/shard_map/all_gather | solution.py:99
  75.7 24.4 %all-gather.3.cloned.1.call-done = f32[4,512,256]{2,0,1:T(4,128)} async-done(((f32[4,16,256]{2,0,1:T(4,128)}), f32[4,512,256]{2,0,1:T(4,128)}) %all-gather.3.cloned.1.call-update) | async-done | bytes 2097168 | tf_op jit(solution)/shard_map/all_gather | solution.py:98
  103.6 65.3 %while.22 = (s32[]{:T(128)}, f32[16,256]{1,0:T(8,128)S(1)}, f32[16,3,256]{2,1,0:T(4,128)S(1)}, f32[16,4,8,256]{3,2,0,1:T(8,128)S(1)}, f32[16,256]{1,0:T(8,128)}) while((s32[]{:T(128)}, f32[16,256]{1,0:T(8,128)S(1)}, f32[16,3,256]{2,1,0:T(4,128)S(1)}, f32[16,4,8,256]{3,2,0,1:T(8,128)S(1)}, f32[16,256]{1,0:T(8,128)}) %tuple.100), condition=%wide.region_2.3_spmd.clone, body=%wide.region_0.2_spmd.sunk.clone | while | flops 13107972 | bytes 247921 | solution.py:106
  169.6 2.9 collective-permute-start.3
  172.6 48.0 %all-gather = f32[512,256]{1,0:T(8,128)S(1)} all-gather(f32[16,256]{1,0:T(8,128)S(1)} %get-tuple-element.355), channel_id=2, replica_groups=mesh['slab'=16,'sub'=32] {'sub'}, dimensions={0}, use_global_device_ids=true | all-gather | bytes 540672 | tf_op jit(solution)/shard_map/all_gather | solution.py:110
  222.5 59.9 %while.23 = (s32[]{:T(128)}, f32[16,3,256]{2,0,1:T(8,128)S(1)}, f32[16,5,8,256]{3,2,1,0:T(8,128)S(1)}, f32[16,256]{1,0:T(8,128)S(1)}, f32[16,3,256]{2,1,0:T(4,128)S(1)}, /*index=5*/f32[16,256]{1,0:T(8,128)}) while((s32[]{:T(128)}, f32[16,3,256]{2,0,1:T(8,128)S(1)}, f32[16,5,8,256]{3,2,1,0:T(8,128)S(1)}, f32[16,256]{1,0:T(8,128)S(1)}, ...), condition=%wide.region_7.8_spmd.clone, body=%wide.region_3.7_spmd.sunk.clone | while | flops 14683398 | bytes 243869 | solution.py:115
  223.4 2.8 fusion.34
  227.1 2.8 fusion.34
  230.8 2.8 fusion.34
  234.6 2.8 fusion.34
  238.3 2.8 fusion.34
  242.1 2.8 fusion.34
  249.6 2.8 fusion.34
  253.3 2.8 fusion.34
  257.0 2.8 fusion.34
  260.8 2.8 fusion.34
  264.5 2.8 fusion.34
  268.3 2.8 fusion.34
  275.7 2.8 fusion.34
  279.5 2.8 fusion.34
  284.9 6.6 %all-to-all-start.1 = ((f32[6,32,8]{2,0,1:T(8,128)}), f32[6,32,8]{2,0,1:T(8,128)S(1)}, u32[]{:S(2)}, u32[]{:S(2)}) async-start(f32[6,32,8]{2,0,1:T(8,128)} %copy.92), calls=%async_computation.1 | async-start | bytes 262144 | tf_op jit(solution)/shard_map/all_to_all | solution.py:122
  292.1 9.8 %all-to-all-done.1 = f32[6,32,8]{2,0,1:T(8,128)S(1)} async-done(((f32[6,32,8]{2,0,1:T(8,128)}), f32[6,32,8]{2,0,1:T(8,128)S(1)}, u32[]{:S(2)}, u32[]{:S(2)}) %all-to-all-start.1) | async-done | bytes 6176 | tf_op jit(solution)/shard_map/all_to_all | solution.py:122
  (424 shorter events, 101.8 us)
Async XLA Ops:
  7.2 92.9 %all-gather.3.cloned.1.call-start = ((), (), s32[]{:S(2)}) async-start(), calls=%async_computation.2 | async-start | bytes 2162688 | tf_op jit(solution)/shard_map/all_gather | solution.py:98
  9.6 92.8 %collective-permute-start = (f32[4,1,256]{2,0,1:T(4,128)S(1)}, f32[4,1,256]{2,0,1:T(4,128)S(1)}, u32[]{:S(2)}, u32[]{:S(2)}) collective-permute-start(f32[4,1,256]{2,0,1:T(4,128)S(1)} %get-tuple-element.164), channel_id=1, source_target_pairs={{0,32},{32,64},{64,96},{96,128},{128,160},{160,192},{192,224},{224... | collective-permute-start | bytes 12296 | tf_op jit(solution)/shard_map/ppermute | solution.py:24
  9.6 92.8 %collective-permute-start.1 = (f32[4,1,256]{2,0,1:T(4,128)S(1)}, f32[4,1,256]{2,0,1:T(4,128)S(1)}, u32[]{:S(2)}, u32[]{:S(2)}) collective-permute-start(f32[4,1,256]{2,0,1:T(4,128)S(1)} %get-tuple-element.165), channel_id=1, source_target_pairs={{32,0},{64,32},{96,64},{128,96},{160,128},{192,160},{224,192},{256... | collective-permute-start | bytes 12296 | tf_op jit(solution)/shard_map/ppermute | solution.py:25
  13.9 61.1 %all-to-all-start = ((s32[1,32,1]{2,0,1:T(1,128)}), s32[1,32,1]{2,0,1:T(1,128)S(1)}, u32[]{:S(2)}, u32[]{:S(2)}) async-start(s32[1,32,1]{2,0,1:T(1,128)} %copy.89), calls=%async_computation | async-start | bytes 32768 | tf_op jit(solution)/shard_map/all_to_all | solution.py:123
  103.5 65.3 %copy-start.2 = (f32[16,256]{1,0:T(8,128)S(1)}, f32[16,256]{1,0:T(8,128)}, u32[]{:S(2)}) copy-start(f32[16,256]{1,0:T(8,128)} %param.18) | copy-start | bytes 49156
  103.5 65.3 %copy-start.3 = (s32[16]{0:T(128)S(1)}, s32[16]{0:T(128)}, u32[]{:S(2)}) copy-start(s32[16]{0:T(128)} %param.19) | copy-start | bytes 196
  169.6 51.7 %collective-permute-start.2 = (f32[1,1,256]{2,0,1:T(1,128)S(1)}, f32[1,1,256]{2,0,1:T(1,128)S(1)}, u32[]{:S(2)}, u32[]{:S(2)}) collective-permute-start(f32[1,1,256]{2,0,1:T(1,128)S(1)} %get-tuple-element.170), channel_id=1, source_target_pairs={{0,32},{32,64},{64,96},{96,128},{128,160},{160,192},{192,224},{224... | collective-permute-start | bytes 3080 | tf_op jit(solution)/shard_map/ppermute | solution.py:24
  169.6 51.7 %collective-permute-start.3 = (f32[1,1,256]{2,0,1:T(1,128)S(1)}, f32[1,1,256]{2,0,1:T(1,128)S(1)}, u32[]{:S(2)}, u32[]{:S(2)}) collective-permute-start(f32[1,1,256]{2,0,1:T(1,128)S(1)} %get-tuple-element.171), channel_id=1, source_target_pairs={{32,0},{64,32},{96,64},{128,96},{160,128},{192,160},{224,192},{256... | collective-permute-start | bytes 3080 | tf_op jit(solution)/shard_map/ppermute | solution.py:25
  222.5 59.9 %copy-start = (f32[3,16,256]{2,1,0:T(8,128)S(1)}, f32[3,16,256]{2,1,0:T(8,128)}, u32[]{:S(2)}) copy-start(f32[3,16,256]{2,1,0:T(8,128)} %param.14) | copy-start | bytes 147460
  222.5 59.9 %copy-start.1 = (f32[3,16,256]{2,1,0:T(8,128)S(1)}, f32[3,16,256]{2,1,0:T(8,128)}, u32[]{:S(2)}) copy-start(f32[3,16,256]{2,1,0:T(8,128)} %param.15) | copy-start | bytes 147460
  284.9 17.1 %all-to-all-start.1 = ((f32[6,32,8]{2,0,1:T(8,128)}), f32[6,32,8]{2,0,1:T(8,128)S(1)}, u32[]{:S(2)}, u32[]{:S(2)}) async-start(f32[6,32,8]{2,0,1:T(8,128)} %copy.92), calls=%async_computation.1 | async-start | bytes 262144 | tf_op jit(solution)/shard_map/all_to_all | solution.py:122
Sparse Core Ops, SparseCore 0:
  11.7 88.3 all-gather.2
where the time goes:
time: 314 us; the launch traced here: 310 us
  other arithmetic  113 us (36%)
  blocking collectives  91.6 us (29%)
  waiting for transfers between devices  34.3 us (11%)
  local copies, waits for them, and re-layouts  27.8 us (9%)
  starting transfers between devices  25.7 us (8%)
  between operations  14.4 us (5%)
    all_gather x1, blocking collectives, on_device(): press_every = lax.all_gather(press_block, 'sub', axis=1, tiled=True)  48 us
    reduce_sum x16, other arithmetic, pair_force(): jnp.sum(factor * apart_x, axis=1)  44.7 us
    all_gather x1, blocking collectives, on_device(): lax.all_gather(send_cells, 'sub', axis=0, tiled=True)  43.6 us
    reduce_sum x16, other arithmetic, pair_density(): jnp.sum(kernel * masses[None, :], axis=1) / (math.pi * own_width ** 3)  39.9 us
    all_gather x1, waiting for transfers between devices, on_device(): lax.all_gather(block, 'sub', axis=1, tiled=True)  24.4 us
    all_to_all x1, starting transfers between devices, on_device(): lax.all_to_all(mig_counts, 'sub', split_axis=1, concat_axis=1, tiled=True)  13.2 us
    dynamic_slice x32, local copies, waits for them, and re-layouts, on_device(): density = lax.map(density_cell, (own_pos, smoothing, nearby))  11.5 us
    mul x16, other arithmetic, pair_force(): return -push / (math.pi * own_width ** 5)  11.4 us
  transfers between devices with their start and end apart: 7, of which 2 were waited for; matrix products, arithmetic and copies ran while one was open for 3% of the time, Pallas kernels for 0%

commit v1 on v0

v1 whole, which is shorter than its diff:
```python
import functools
import math

import jax
import jax.numpy as jnp
from jax import lax
from jax.experimental import pallas as pl
from jax.experimental.pallas import tpu as pltpu
from jax.sharding import PartitionSpec as P

P_SIZE = 256
HALF = 128
M = 8
K_ROWS = 48
V_ROWS = 32
ROW_BLOCK = 32
SIZES = (128, 160, 192, 224, 256)
TINY = 1e-12

adiabatic = 5.0 / 3.0
time_step = 0.05

VMEM = pl.BlockSpec(memory_space=pltpu.VMEM)
SMEM = pl.BlockSpec(memory_space=pltpu.SMEM)
PARAMS = pltpu.CompilerParams(vmem_limit_bytes=56 * 1024 * 1024)


def split(value):
    high = value.astype(jnp.bfloat16).astype(jnp.float32)
    rest = value - high
    mid = rest.astype(jnp.bfloat16).astype(jnp.float32)
    return high, mid, rest - mid


def row_ids():
    return lax.broadcasted_iota(jnp.int32, (8, HALF), 0)


def half_rows(record, half):
    return record if half == 0 else pltpu.roll(record, 4, 0)


def norms(tile, row):
    square = tile * tile
    return (
        pltpu.roll(square, row, 0) + pltpu.roll(square, row - 1, 0) + pltpu.roll(square, row - 2, 0)
    )


def right_operand(record):
    rows = row_ids()
    parts = []
    for half in range(2):
        tile = half_rows(record, half)
        feature = jnp.where(rows < 4, tile, 0.0)
        feature = jnp.where(rows == 4, norms(tile, 4), feature)
        feature = jnp.where(rows == 5, 1.0, feature)
        high, mid, low = split(feature)
        parts.append(jnp.concatenate([high, high, mid, high, low, mid], axis=0))
    return jnp.concatenate(parts, axis=1).astype(jnp.bfloat16)


def left_operand(record, width):
    rows = row_ids()
    parts = []
    for half in range(2):
        tile = half_rows(record, half)
        h = width[:, half * HALF : (half + 1) * HALF]
        scale = jnp.broadcast_to(1.0 / (h * h), (8, HALF))
        feature = jnp.where(rows < 3, -2.0 * scale * tile, 0.0)
        feature = jnp.where(rows == 4, scale, feature)
        feature = jnp.where(rows == 5, scale * norms(tile, 5), feature)
        high, mid, low = split(feature)
        pad = jnp.zeros((HALF - K_ROWS, HALF), jnp.float32)
        parts.append(jnp.concatenate([high, mid, high, low, high, mid, pad], axis=0).T)
    return jnp.concatenate(parts, axis=0).astype(jnp.bfloat16)


def pack_kernel(counts, send, pos, mass, rec, out):
    cells = mass.shape[0]
    lane = lax.broadcasted_iota(jnp.int32, (1, P_SIZE), 1)
    for c in range(cells):
        live = lane < counts[c]
        for k in range(4):
            row = pos[k, c : c + 1, :] - 0.5 if k < 3 else mass[c : c + 1, :]
            row = jnp.where(live, row, 0.0)
            rec[c, k : k + 1, :] = row[:, :HALF]
            rec[c, k + 4 : k + 5, :] = row[:, HALF:]
    for v in range(out.shape[0]):
        for k in range(send.shape[0]):
            out[v, 8 * k : 8 * k + 8, :] = rec[send[k, v]]


def fill_table(rec, rim_lo, rim_hi, recv, table):
    cells = rec.shape[0]
    table[0] = rim_lo[0]
    for c in range(cells):
        table[1 + c] = rec[c]
    table[cells + 1] = rim_hi[0]
    peers = recv.shape[0]
    per_peer = recv.shape[1] // 8
    for v in range(peers):
        for k in range(per_peer):
            table[cells + 2 + v * per_peer + k] = recv[v, 8 * k : 8 * k + 8, :]


def fill_operands(table, rec, smoothing, right, left):
    def table_step(t, carry):
        right[t] = right_operand(table[t])
        return carry

    lax.fori_loop(0, table.shape[0], table_step, 0, unroll=2)
    for c in range(rec.shape[0]):
        left[c] = left_operand(rec[c], smoothing[c : c + 1, :])


def by_size(count, run):
    for k, size in enumerate(SIZES):
        below = SIZES[k - 1] if k else -1
        pl.when((count > below) & (count <= size))(functools.partial(run, size))


def density_kernel(
    counts, partners, send, rec, rim_lo, rim_hi, recv, smoothing, energy,
    density, press, press_rec, press_send,
    table, right, left, square, total,
):
    cells = rec.shape[0]
    pairs = partners.shape[0]
    fill_table(rec, rim_lo, rim_hi, recv, table)
    fill_operands(table, rec, smoothing, right, left)

    def cell(c, carry):
        def run(size):
            def product(p):
                square[p % 2, :size, :] = jnp.dot(
                    left[c, :size, :K_ROWS], right[partners[p, c]], preferred_element_type=jnp.float32
                )

            product(0)
            for p in range(pairs):
                if p + 1 < pairs:
                    product(p + 1)
                t = partners[p, c]
                masses = (table[t, 3:4, :], table[t, 7:8, :])
                for base in range(0, size, ROW_BLOCK):
                    block = pl.ds(base, ROW_BLOCK)
                    term = 0.0
                    for half in range(2):
                        s = jnp.maximum(square[p % 2, block, half * HALF : (half + 1) * HALF], TINY)
                        q = s * lax.rsqrt(s)
                        outer = jnp.maximum(2.0 - q, 0.0)
                        inner = jnp.maximum(outer - 1.0, 0.0)
                        w = 0.25 * (outer * outer * outer) - inner * inner * inner
                        term = term + w * masses[half]
                    total[c, block, :] = term if p == 0 else total[c, block, :] + term
            if size < P_SIZE:
                total[c, size:, :] = jnp.zeros((P_SIZE - size, HALF), jnp.float32)

        by_size(counts[c], run)
        return carry

    lax.fori_loop(0, cells, cell, 0)

    ones = jnp.ones((8, HALF), jnp.float32)
    lane = lax.broadcasted_iota(jnp.int32, (1, P_SIZE), 1)
    for c in range(cells):
        summed = lax.dot_general(
            ones, total[c], (((1,), (1,)), ((), ())),
            precision=lax.Precision.HIGHEST, preferred_element_type=jnp.float32,
        )[0:1, :]
        width = smoothing[c : c + 1, :]
        live = lane < counts[c]
        rho = summed / (math.pi * width * width * width)
        density[c : c + 1, :] = jnp.where(live, rho, 0.0)
        value = jnp.where(
            live, (adiabatic - 1.0) * energy[c : c + 1, :] / jnp.where(live, rho, 1.0), 0.0
        )
        press[c : c + 1, :] = value
        press_rec[c, 0:1, :] = value[:, :HALF]
        press_rec[c, 1:2, :] = value[:, HALF:]
    for v in range(send.shape[1]):
        for k in range(send.shape[0]):
            press_send[v, 2 * k : 2 * k + 2, :] = press_rec[send[k, v]]


def force_kernel(
    counts, partners, rec, rim_lo, rim_hi, recv, smoothing, press_rec, press_lo, press_hi, press_recv,
    pos, vel, press, picks,
    state, leaving,
    table, right, left, press_table, weights, square, slope_high, slope_low, total,
):
    cells = rec.shape[0]
    pairs = partners.shape[0]
    fill_table(rec, rim_lo, rim_hi, recv, table)
    fill_operands(table, rec, smoothing, right, left)
    press_table[0] = press_lo[0]
    for c in range(cells):
        press_table[1 + c] = press_rec[c]
    press_table[cells + 1] = press_hi[0]
    per_peer = press_recv.shape[1] // 2
    for v in range(press_recv.shape[0]):
        for k in range(per_peer):
            press_table[cells + 2 + v * per_peer + k] = press_recv[v, 2 * k : 2 * k + 2, :]

    def weight_step(t, carry):
        rows = row_ids()
        parts = []
        for half in range(2):
            tile = half_rows(table[t], half)
            mass = jnp.broadcast_to(tile[3:4, :], (8, HALF))
            one = jnp.where(rows == 3, 1.0, jnp.where(rows < 4, tile, 0.0))
            both = jnp.where(rows < 4, one, pltpu.roll(one, 4, 0) * press_table[t, half : half + 1, :])
            high, mid, low = split(both * mass)
            parts.append(jnp.concatenate([high, mid, low, jnp.zeros_like(low)], axis=0))
        weights[t] = jnp.concatenate(parts, axis=1).astype(jnp.bfloat16)
        return carry

    lax.fori_loop(0, table.shape[0], weight_step, 0, unroll=2)
    lane = lax.broadcasted_iota(jnp.int32, (1, P_SIZE), 1)

    def cell(c, carry):
        def run(size):
            def product(p):
                square[p % 2, :size, :] = jnp.dot(
                    left[c, :size, :K_ROWS], right[partners[p, c]], preferred_element_type=jnp.float32
                )

            def gather(p):
                w = weights[partners[p, c]]
                dims = (((1,), (1,)), ((), ()))
                added = lax.dot_general(
                    slope_high[p % 2, :size, :], w, dims, preferred_element_type=jnp.float32
                ) + lax.dot_general(
                    slope_low[p % 2, :size, :], w, dims, preferred_element_type=jnp.float32
                )
                old = total[:size, :V_ROWS]
                total[:size, :V_ROWS] = added if p == 0 else old + added

            product(0)
            for p in range(pairs):
                if p + 1 < pairs:
                    product(p + 1)
                if p:
                    gather(p - 1)
                for base in range(0, size, ROW_BLOCK):
                    block = pl.ds(base, ROW_BLOCK)
                    s = jnp.maximum(square[p % 2, block, :], TINY)
                    y = lax.rsqrt(s)
                    q = jnp.minimum(s * y, 2.0)
                    inverse = jnp.minimum(jnp.maximum(y, 0.5), 1.0)
                    f = (inverse - 1.0) + (jnp.maximum(q, 1.0) - 0.75 * q)
                    high = f.astype(jnp.bfloat16)
                    slope_high[p % 2, block, :] = high
                    slope_low[p % 2, block, :] = (f - high.astype(jnp.float32)).astype(jnp.bfloat16)
            gather(pairs - 1)

        by_size(counts[c], run)
        sums = total[...].T
        sums = sums[0:8, :] + sums[8:16, :] + sums[16:24, :]
        width = smoothing[pl.ds(c, 1), :]
        squared = width * width
        factor = (3.0 * time_step / math.pi) / (squared * squared * width)
        own = press[pl.ds(c, 1), :]
        live = lane < counts[c]
        for k in range(3):
            place = pos[k, pl.ds(c, 1), :]
            centred = place - 0.5
            push = own * (centred * sums[3:4, :] - sums[k : k + 1, :]) + (
                centred * sums[7:8, :] - sums[4 + k : 5 + k, :]
            )
            speed = vel[k, pl.ds(c, 1), :] + factor * push
            state[k, pl.ds(c, 1), :] = jnp.where(live, place + time_step * speed, 0.0)
            state[3 + k, pl.ds(c, 1), :] = jnp.where(live, speed, 0.0)
        return carry

    lax.fori_loop(0, cells, cell, 0)

    picked = picks[...]
    in_cell = picked % P_SIZE
    of_cell = picked // P_SIZE
    chosen = lax.broadcasted_iota(jnp.int32, (P_SIZE, P_SIZE), 0) == in_cell
    chosen = jnp.where(chosen, 1.0, 0.0).astype(jnp.bfloat16)
    mine = lax.broadcasted_iota(jnp.int32, (cells, P_SIZE), 0) == of_cell
    for k in range(6):
        found = 0.0
        for part in split(state[k]):
            found = found + jnp.dot(part.astype(jnp.bfloat16), chosen, preferred_element_type=jnp.float32)
        leaving[k : k + 1, :] = jnp.sum(jnp.where(mine, found, 0.0), axis=0, keepdims=True)


def neighbours(value, axis):
    count = lax.axis_size(axis)
    up = [(i, (i + 1) % count) for i in range(count)]
    down = [(j, i) for i, j in up]
    return lax.ppermute(value[-1:], axis, up), lax.ppermute(value[:1], axis, down)


def exchange(value):
    return lax.all_to_all(value, "sub", split_axis=0, concat_axis=0, tiled=True)


def on_device(
    positions, velocities, mass, smoothing, energy, cell_counts, send_cells, partners, mig_list, mig_counts
):
    cells = mass.shape[0]
    peers = lax.axis_size("sub")
    kept = send_cells.shape[2]
    width = cells + 2 + peers * kept
    f32 = jnp.float32
    send = send_cells[0].T
    links = partners.T
    rec, outgoing = pl.pallas_call(
        pack_kernel,
        out_shape=(
            jax.ShapeDtypeStruct((cells, 8, HALF), f32),
            jax.ShapeDtypeStruct((peers, 8 * kept, HALF), f32),
        ),
        in_specs=[SMEM, SMEM, VMEM, VMEM],
        out_specs=(VMEM, VMEM),
        compiler_params=PARAMS,
    )(cell_counts, send, positions, mass)
    recv = exchange(outgoing)
    rim_lo, rim_hi = neighbours(rec, "slab")

    keep = jnp.arange(M)[None, :] < mig_counts[0][:, None]
    picks = jnp.where(keep, mig_list[0], -P_SIZE).reshape(1, peers * M)

    tables = [
        pltpu.VMEM((width, 8, HALF), f32),
        pltpu.VMEM((width, K_ROWS, P_SIZE), jnp.bfloat16),
        pltpu.VMEM((cells, P_SIZE, HALF), jnp.bfloat16),
    ]
    density, press, press_rec, press_out = pl.pallas_call(
        density_kernel,
        out_shape=(
            jax.ShapeDtypeStruct((cells, P_SIZE), f32),
            jax.ShapeDtypeStruct((cells, P_SIZE), f32),
            jax.ShapeDtypeStruct((cells, 2, HALF), f32),
            jax.ShapeDtypeStruct((peers, 2 * kept, HALF), f32),
        ),
        in_specs=[SMEM] * 3 + [VMEM] * 6,
        out_specs=(VMEM,) * 4,
        scratch_shapes=tables
        + [pltpu.VMEM((2, P_SIZE, P_SIZE), f32), pltpu.VMEM((cells, P_SIZE, HALF), f32)],
        compiler_params=PARAMS,
    )(cell_counts, links, send, rec, rim_lo, rim_hi, recv, smoothing, energy)
    press_recv = exchange(press_out)
    press_lo, press_hi = neighbours(press_rec, "slab")

    state, leaving = pl.pallas_call(
        force_kernel,
        out_shape=(
            jax.ShapeDtypeStruct((6, cells, P_SIZE), f32),
            jax.ShapeDtypeStruct((6, peers * M), f32),
        ),
        in_specs=[SMEM] * 2 + [VMEM] * 13,
        out_specs=(VMEM, VMEM),
        scratch_shapes=tables
        + [
            pltpu.VMEM((width, 2, HALF), f32),
            pltpu.VMEM((width, V_ROWS, P_SIZE), jnp.bfloat16),
            pltpu.VMEM((2, P_SIZE, P_SIZE), f32),
            pltpu.VMEM((2, P_SIZE, P_SIZE), jnp.bfloat16),
            pltpu.VMEM((2, P_SIZE, P_SIZE), jnp.bfloat16),
            pltpu.VMEM((P_SIZE, HALF), f32),
        ],
        compiler_params=PARAMS,
    )(
        cell_counts, links, rec, rim_lo, rim_hi, recv, smoothing, press_rec, press_lo, press_hi, press_recv,
        positions, velocities, press, picks,
    )
    arrived = lax.all_to_all(leaving.reshape(6, peers, M), "sub", split_axis=1, concat_axis=1, tiled=True)
    return density, state, arrived.reshape(6, peers * M)


def solution(mesh):
    both = ("slab", "sub")
    return jax.shard_map(
        on_device,
        mesh=mesh,
        in_specs=(
            P(None, both, None),
            P(None, both, None),
            P(both, None),
            P(both, None),
            P(both, None),
            P(both),
            P(both, None, None),
            P(both, None),
            P(both, None, None),
            P(both, None),
        ),
        out_specs=(P(both, None), P(None, both, None), P(None, both)),
        check_vma=False,
    )
```

time: 314 us -> 111 us (0.35); the launches traced: 310 us -> 110 us
  other arithmetic: 113 us -> 0.65 us
  blocking collectives: 91.6 us -> 14 us
  Pallas kernels: 0 us -> 49.3 us
  local copies, waits for them, and re-layouts: 27.8 us -> 4.54 us
  waiting for transfers between devices: 34.3 us -> 17.9 us
  between operations: 14.4 us -> 0.71 us
    all_gather x2 -> x0, blocking collectives: 91.6 us -> none  [the longest x1 48 us: on_device(): press_every = lax.all_gather(press_block, 'sub', axis=1, tiled=True)]
    reduce_sum x32 -> x0, other arithmetic: 84.6 us -> none  [the longest x16 44.7 us: pair_force(): jnp.sum(factor * apart_x, axis=1)]
    pallas_call x0 -> x3, Pallas kernels: none -> 49.3 us  [the longest x1 25.7 us: on_device(): pl.pallas_call(force_kernel, out_shape=(jax.ShapeDtypeStruct((6, cells, P...]
    all_gather x1 -> x0, waiting for transfers between devices: 24.4 us -> none  [on_device(): lax.all_gather(block, 'sub', axis=1, tiled=True)]
    all_to_all x0 -> x1, blocking collectives: none -> 14 us  [on_device(): lax.all_to_all(leaving.reshape(6, peers, M), 'sub', split_axis=1, concat_...]
    dynamic_slice x33 -> x0, local copies, waits for them, and re-layouts: 12.2 us -> none  [the longest x32 11.5 us: on_device(): density = lax.map(density_cell, (own_pos, smoothing, nearby))]
    div x32 -> x0, other arithmetic: 11.6 us -> none  [the longest x16 11.4 us: pair_density(): jnp.sum(kernel * masses[None, :], axis=1) / (math.pi * own_width ** 3)]
    mul x17 -> x0, other arithmetic: 11.4 us -> none  [the longest x16 11.4 us: pair_force(): return -push / (math.pi * own_width ** 5)]
  transfers between devices with their start and end apart: 7 -> 6, of which waited for: 2 -> 3; matrix products, arithmetic and copies ran while one was open for 3% -> 1% of each run, Pallas kernels for 0% -> 0%
where the time goes in v1:
time: 111 us; the launch traced here: 110 us
  Pallas kernels  49.3 us (44%)
  starting transfers between devices  23.1 us (21%)
  waiting for transfers between devices  17.9 us (16%)
  blocking collectives  14 us (13%)
  local copies, waits for them, and re-layouts  4.54 us (4%)
    pallas_call x1, Pallas kernels, on_device(): pl.pallas_call(force_kernel, out_shape=(jax.ShapeDtypeStruct((6, cells, P...  25.7 us
    pallas_call x1, Pallas kernels, on_device(): pl.pallas_call(density_kernel, out_shape=(jax.ShapeDtypeStruct((cells, P_...  22 us
    all_to_all x2, starting transfers between devices, exchange(): return lax.all_to_all(value, 'sub', split_axis=0, concat_axis=0, tiled=True)  17.2 us
    all_to_all x2, waiting for transfers between devices, exchange(): return lax.all_to_all(value, 'sub', split_axis=0, concat_axis=0, tiled=True)  16.9 us
    all_to_all x1, blocking collectives, on_device(): lax.all_to_all(leaving.reshape(6, peers, M), 'sub', split_axis=1, concat_...  14 us
    ppermute x2, starting transfers between devices, neighbours(): lax.ppermute(value[:1], axis, down)  5.91 us
  transfers between devices with their start and end apart: 6, of which 3 were waited for; matrix products, arithmetic and copies ran while one was open for 1% of the time, Pallas kernels for 0%

profile of v1, /device:TPU:32, one launch (start us, length us, event | category | flops | bytes accessed | tf_op | source)
XLA Modules:
  0.0 110.2 jit_solution(16374933572824559712)
XLA Ops:
  0.6 1.7 %shard_map.121 = (f32[16,8,128]{2,1,0:T(8,128)}, f32[32,16,128]{2,1,0:T(8,128)}) custom-call(s32[16]{0:T(128)} %counts.5, s32[2,32]{1,0:T(2,128)} %bitcast.7, f32[3,16,256]{2,1,0:T(8,128)} %pos.3, f32[16,256]{1,0:T(8,128)} %mass.1), custom_call_target="tpu_custom_call" | custom-call | tf_op jit(solution)/shard_map/pallas_call | solution.py:313
  2.3 13.2 %all-to-all-start = ((f32[32,16,128]{2,1,0:T(8,128)}), f32[32,16,128]{2,1,0:T(8,128)S(1)}, u32[]{:S(2)}, u32[]{:S(2)}) async-start(f32[32,16,128]{2,1,0:T(8,128)} %get-tuple-element.12), calls=%async_computation | async-start | bytes 524288 | tf_op jit(solution)/shard_map/all_to_all | solution.py:300
  15.5 0.7 fusion
  16.2 3.0 %collective-permute-start.1 = (f32[1,8,128]{2,1,0:T(8,128)S(1)}, f32[1,8,128]{2,1,0:T(8,128)S(1)}, u32[]{:S(2)}, u32[]{:S(2)}) collective-permute-start(f32[1,8,128]{2,1,0:T(8,128)S(1)} %get-tuple-element.19), channel_id=1, source_target_pairs={{32,0},{64,32},{96,64},{128,96},{160,128},{192,160},{224,192},{256... | collective-permute-start | bytes 12296 | tf_op jit(solution)/shard_map/ppermute | solution.py:296
  19.1 0.1 iota_compare_fusion
  19.2 0.1 copy.15
  19.3 0.1 squeeze.7
  19.4 0.1 lt.29
  19.5 0.9 collective-permute-done.rim_lo
  20.4 0.0 collective-permute-done.1.rim_hi
  20.5 7.7 %all-to-all-done.recv = f32[32,16,128]{2,1,0:T(8,128)S(1)} async-done(((f32[32,16,128]{2,1,0:T(8,128)}), f32[32,16,128]{2,1,0:T(8,128)S(1)}, u32[]{:S(2)}, u32[]{:S(2)}) %all-to-all-start) | async-done | bytes 262176 | tf_op jit(solution)/shard_map/all_to_all | solution.py:300
  28.2 0.7 copy-done
  28.8 22.0 %shard_map.122 = (f32[16,256]{1,0:T(8,128)}, f32[16,256]{1,0:T(8,128)}, f32[16,2,128]{2,1,0:T(2,128)}, f32[32,4,128]{2,1,0:T(4,128)}) custom-call(s32[16]{0:T(128)} %counts.5, s32[8,16]{1,0:T(8,128)} %bitcast.5, s32[2,32]{1,0:T(2,128)} %bitcast.8, f32[16,8,128]{2,1,0:T(8,128)} %get-tuple-element.11.rec, f32[1,8,128]{2,1,0:T(8,128)} %copy-done.2, ...), custom_call_target="tpu_custom_call" | custom-call | tf_op jit(solution)/shard_map/pallas_call | solution.py:334
  50.8 0.7 fusion.1
  51.5 3.0 %collective-permute-start.3 = (f32[1,2,128]{2,1,0:T(2,128)S(1)}, f32[1,2,128]{2,1,0:T(2,128)S(1)}, u32[]{:S(2)}, u32[]{:S(2)}) collective-permute-start(f32[1,2,128]{2,1,0:T(2,128)S(1)} %get-tuple-element.21), channel_id=1, source_target_pairs={{32,0},{64,32},{96,64},{128,96},{160,128},{192,160},{224,192},{256... | collective-permute-start | bytes 3080 | tf_op jit(solution)/shard_map/ppermute | solution.py:296
  54.5 4.0 %all-to-all-start.1 = ((f32[32,4,128]{2,1,0:T(4,128)}), f32[32,4,128]{2,1,0:T(4,128)S(1)}, u32[]{:S(2)}, u32[]{:S(2)}) async-start(f32[32,4,128]{2,1,0:T(4,128)} %get-tuple-element.15), calls=%async_computation.1 | async-start | bytes 131072 | tf_op jit(solution)/shard_map/all_to_all | solution.py:300
  58.5 0.6 broadcast_select_fusion.picks
  59.1 9.2 %all-to-all-done.1.press_recv = f32[32,4,128]{2,1,0:T(4,128)S(1)} async-done(((f32[32,4,128]{2,1,0:T(4,128)}), f32[32,4,128]{2,1,0:T(4,128)S(1)}, u32[]{:S(2)}, u32[]{:S(2)}) %all-to-all-start.1) | async-done | bytes 65568 | tf_op jit(solution)/shard_map/all_to_all | solution.py:300
  68.4 0.6 copy-done.1
  69.0 25.7 %shard_map.123 = (f32[6,16,256]{2,1,0:T(8,128)}, f32[6,256]{1,0:T(8,128)}) custom-call(s32[16]{0:T(128)} %counts.5, s32[8,16]{1,0:T(8,128)} %bitcast.6, f32[16,8,128]{2,1,0:T(8,128)} %get-tuple-element.11.rec, f32[1,8,128]{2,1,0:T(8,128)} %copy-done.2, f32[1,8,128]{2,1,0:T(8,128)} %copy-done.3, f32[32,16,128]{2,1,0:T(8,128)} %copy-done, ...), custom_call_target="tpu_custom_call" | custom-call | tf_op jit(solution)/shard_map/pallas_call | solution.py:351
  94.7 0.8 reshape.46
  95.5 0.1 copy.16
  95.5 14.0 %all_to_all.15 = f32[6,32,8]{2,0,1:T(8,128)S(1)} all-to-all(f32[6,32,8]{2,0,1:T(8,128)S(1)} %copy.16), channel_id=1, replica_groups=mesh['slab'=16,'sub'=32] {'sub'}, dimensions={1} | all-to-all | bytes 12288 | tf_op jit(solution)/shard_map/all_to_all | solution.py:373
  109.5 0.7 reshape.47
  (19 shorter events, 0.1 us)
Async XLA Ops:
  2.3 25.9 %all-to-all-start = ((f32[32,16,128]{2,1,0:T(8,128)}), f32[32,16,128]{2,1,0:T(8,128)S(1)}, u32[]{:S(2)}, u32[]{:S(2)}) async-start(f32[32,16,128]{2,1,0:T(8,128)} %get-tuple-element.12), calls=%async_computation | async-start | bytes 524288 | tf_op jit(solution)/shard_map/all_to_all | solution.py:300
  15.5 3.7 %copy-start.7 = (s32[1,32]{1,0:T(1,128)S(1)}, s32[1,32]{1,0:T(1,128)}, u32[]{:S(2)}) copy-start(s32[1,32]{1,0:T(1,128)} %param.19) | copy-start | bytes 388
  16.2 3.0 %copy-start.4 = (s32[1,32,8]{1,2,0:T(8,128)S(1)}, s32[1,32,8]{1,2,0:T(8,128)}, u32[]{:S(2)}) copy-start(s32[1,32,8]{1,2,0:T(8,128)} %param.18) | copy-start | bytes 3076
  16.2 4.2 %collective-permute-start = (f32[1,8,128]{2,1,0:T(8,128)S(1)}, f32[1,8,128]{2,1,0:T(8,128)S(1)}, u32[]{:S(2)}, u32[]{:S(2)}) collective-permute-start(f32[1,8,128]{2,1,0:T(8,128)S(1)} %get-tuple-element.20), channel_id=1, source_target_pairs={{0,32},{32,64},{64,96},{96,128},{128,160},{160,192},{192,224},{224... | collective-permute-start | bytes 12296 | tf_op jit(solution)/shard_map/ppermute | solution.py:296
  16.2 4.3 %collective-permute-start.1 = (f32[1,8,128]{2,1,0:T(8,128)S(1)}, f32[1,8,128]{2,1,0:T(8,128)S(1)}, u32[]{:S(2)}, u32[]{:S(2)}) collective-permute-start(f32[1,8,128]{2,1,0:T(8,128)S(1)} %get-tuple-element.19), channel_id=1, source_target_pairs={{32,0},{64,32},{96,64},{128,96},{160,128},{192,160},{224,192},{256... | collective-permute-start | bytes 12296 | tf_op jit(solution)/shard_map/ppermute | solution.py:296
  20.4 7.7 %copy-start.2 = (f32[1,8,128]{2,1,0:T(8,128)}, f32[1,8,128]{2,1,0:T(8,128)S(1)}, u32[]{:S(2)}) copy-start(f32[1,8,128]{2,1,0:T(8,128)S(1)} %collective-permute-done.rim_lo) | copy-start | bytes 12292
  20.5 7.7 %copy-start.3 = (f32[1,8,128]{2,1,0:T(8,128)}, f32[1,8,128]{2,1,0:T(8,128)S(1)}, u32[]{:S(2)}) copy-start(f32[1,8,128]{2,1,0:T(8,128)S(1)} %collective-permute-done.1.rim_hi) | copy-start | bytes 12292
  28.1 0.7 copy-start
  51.5 7.6 %collective-permute-start.2 = (f32[1,2,128]{2,1,0:T(2,128)S(1)}, f32[1,2,128]{2,1,0:T(2,128)S(1)}, u32[]{:S(2)}, u32[]{:S(2)}) collective-permute-start(f32[1,2,128]{2,1,0:T(2,128)S(1)} %get-tuple-element.22), channel_id=1, source_target_pairs={{0,32},{32,64},{64,96},{96,128},{128,160},{160,192},{192,224},{224... | collective-permute-start | bytes 3080 | tf_op jit(solution)/shard_map/ppermute | solution.py:296
  51.5 7.6 %collective-permute-start.3 = (f32[1,2,128]{2,1,0:T(2,128)S(1)}, f32[1,2,128]{2,1,0:T(2,128)S(1)}, u32[]{:S(2)}, u32[]{:S(2)}) collective-permute-start(f32[1,2,128]{2,1,0:T(2,128)S(1)} %get-tuple-element.21), channel_id=1, source_target_pairs={{32,0},{64,32},{96,64},{128,96},{160,128},{192,160},{224,192},{256... | collective-permute-start | bytes 3080 | tf_op jit(solution)/shard_map/ppermute | solution.py:296
  54.5 13.9 %all-to-all-start.1 = ((f32[32,4,128]{2,1,0:T(4,128)}), f32[32,4,128]{2,1,0:T(4,128)S(1)}, u32[]{:S(2)}, u32[]{:S(2)}) async-start(f32[32,4,128]{2,1,0:T(4,128)} %get-tuple-element.15), calls=%async_computation.1 | async-start | bytes 131072 | tf_op jit(solution)/shard_map/all_to_all | solution.py:300
  59.1 9.3 %copy-start.5 = (f32[1,2,128]{2,1,0:T(2,128)}, f32[1,2,128]{2,1,0:T(2,128)S(1)}, u32[]{:S(2)}) copy-start(f32[1,2,128]{2,1,0:T(2,128)S(1)} %collective-permute-done.2.press_lo) | copy-start | bytes 3076
  59.1 9.3 %copy-start.6 = (f32[1,2,128]{2,1,0:T(2,128)}, f32[1,2,128]{2,1,0:T(2,128)S(1)}, u32[]{:S(2)}) copy-start(f32[1,2,128]{2,1,0:T(2,128)S(1)} %collective-permute-done.3.press_hi) | copy-start | bytes 3076
  68.4 0.6 copy-start.1

commit v2 on v0

v2 whole, which is shorter than its diff:
```python
import functools
import math

import jax
import jax.numpy as jnp
from jax import lax
from jax.experimental import pallas as pl
from jax.experimental.pallas import tpu as pltpu
from jax.sharding import PartitionSpec as P

P_SIZE = 256
HALF = 128
M = 8
NEAR = 2
K_ROWS = 32
V_ROWS = 32
STEP = 16
SIZES = tuple(range(128, P_SIZE + 1, STEP))
TINY = 1e-12
MASS_SCALE = 1024.0

adiabatic = 5.0 / 3.0
time_step = 0.05

f32 = jnp.float32
bf16 = jnp.bfloat16
VMEM = pl.BlockSpec(memory_space=pltpu.VMEM)
SMEM = pl.BlockSpec(memory_space=pltpu.SMEM)
LAST = (((1,), (1,)), ((), ()))
FIRST = (((0,), (0,)), ((), ()))


def dot(a, b, dims=(((1,), (0,)), ((), ()))):
    return lax.dot_general(a, b, dims, preferred_element_type=f32)


def shape(*dims):
    return jax.ShapeDtypeStruct(dims, f32)


def split(value):
    high = value.astype(bf16).astype(f32)
    rest = value - high
    mid = rest.astype(bf16).astype(f32)
    return high, mid, rest - mid


def row_ids():
    return lax.broadcasted_iota(jnp.int32, (8, HALF), 0)


def lanes():
    return lax.broadcasted_iota(jnp.int32, (1, P_SIZE), 1)


def swap(tile):
    return pltpu.roll(tile, 4, 0)


def is_fourth():
    return row_ids() % 4 == 3


def norms(tile):
    square = tile * tile
    return pltpu.roll(square, 1, 0) + pltpu.roll(square, 2, 0) + pltpu.roll(square, 3, 0)


def spread_fourth(tile):
    tile = jnp.where(is_fourth(), tile, 0.0)
    tile = tile + pltpu.roll(tile, 7, 0)
    return tile + pltpu.roll(tile, 6, 0)


def halves(first, second):
    top = row_ids() < 4
    return jnp.where(top, first, swap(second)), jnp.where(top, swap(first), second)


def by_row(parts):
    rows = row_ids()
    tile = 0.0
    for k, part in reversed(list(enumerate(parts))):
        tile = jnp.where(rows == k, part, tile)
    return tile


def right_operand(record, weighted):
    rows = row_ids()
    feature = jnp.where(is_fourth(), norms(record), record)
    if weighted:
        root = spread_fourth(record)
        feature = feature * (root * root)
    high, mid, low = split(feature)
    tiles = [halves(high, high), halves(mid, high), halves(low, mid)]
    if weighted:
        ones = []
        for value in halves(root * root, root * root):
            h, m, l = split(value)
            ones.append(jnp.where(rows < 3, h, jnp.where(rows < 5, m, jnp.where(rows < 6, l, 0.0))))
    else:
        ones = [jnp.where(rows < 3, 1.0, 0.0)] * 2
    parts = [jnp.concatenate([tile[k] for tile in tiles] + [ones[k]], axis=0) for k in range(2)]
    return jnp.concatenate(parts, axis=1).astype(bf16)


def left_operand(record, width):
    scale = 1.0 / (width * width)
    scale = jnp.where(row_ids() < 4, scale[:, :HALF], scale[:, HALF:])
    feature = scale * jnp.where(is_fourth(), 1.0, -2.0 * record)
    high, mid, low = split(feature)
    first, second = halves(high, mid), halves(high, low)
    own = spread_fourth(scale * norms(record))
    parts = []
    for k, value in enumerate(halves(own, own)):
        h, m, l = split(value)
        one = by_row([h, m, l, h, m, h])
        pad = jnp.zeros((HALF - K_ROWS, HALF), f32)
        parts.append(jnp.concatenate([first[k], second[k], first[k], one, pad], axis=0).T)
    return jnp.concatenate(parts, axis=0).astype(bf16)


def weight_operand(record, press):
    root = spread_fourth(record)
    plain = jnp.where(is_fourth(), 1.0, record) * (root * root * root * (1.0 / MASS_SCALE))
    pressed = plain * jnp.where(row_ids() < 4, press[0:1, :], press[1:2, :])
    tiles = [halves(*pair) for pair in zip(split(plain), split(pressed))]
    blank = jnp.zeros((8, HALF), f32)
    parts = [jnp.concatenate([tile[k] for tile in tiles] + [blank], axis=0) for k in range(2)]
    return jnp.concatenate(parts, axis=1).astype(bf16)


def sort_cells(counts, order, starts):
    cells = order.shape[0]
    kinds = [jnp.maximum(lax.div(counts[c] + (STEP - 1), STEP) - SIZES[0] // STEP, 0) for c in range(cells)]
    for c in range(cells):
        place = 0
        for other in range(cells):
            if other != c:
                ahead = kinds[other] <= kinds[c] if other < c else kinds[other] < kinds[c]
                place = place + ahead.astype(jnp.int32)
        order[place] = jnp.int32(c)
    for k in range(starts.shape[0]):
        starts[k] = sum((kind < k).astype(jnp.int32) for kind in kinds)


def pack_kernel(counts, send, pos, mass, rec, first, last, out, order, starts):
    cells = mass.shape[0]
    sort_cells(counts, order, starts)
    scaled = mass[...] * MASS_SCALE
    root = jnp.exp(jnp.log(scaled) * (1.0 / 3.0))
    for _ in range(2):
        root = root - (root * root * root - scaled) / (3.0 * root * root)
    for c in range(cells):
        live = lanes() < counts[c]
        for k in range(4):
            row = pos[k, c : c + 1, :] - 0.5 if k < 3 else root[c : c + 1, :]
            row = jnp.where(live, row, 0.0)
            rec[c, k : k + 1, :] = row[:, :HALF]
            rec[c, k + 4 : k + 5, :] = row[:, HALF:]
    first[0] = rec[0]
    last[0] = rec[cells - 1]
    for v in range(out.shape[0]):
        for k in range(send.shape[0]):
            out[v, 8 * k : 8 * k + 8, :] = rec[send[k, v]]


def fill_table(table, rec, rim_lo, rim_hi, recv, rows):
    cells = rec.shape[0]
    table[0] = rim_lo[0]
    for c in range(cells):
        table[1 + c] = rec[c]
    table[cells + 1] = rim_hi[0]
    if recv is not None:
        per_peer = recv.shape[1] // rows
        for v in range(recv.shape[0]):
            for k in range(per_peer):
                table[cells + 2 + v * per_peer + k] = recv[v, rows * k : rows * k + rows, :]


def for_cells(count, step):
    unroll = 4
    done = count - count % unroll

    def body(t, carry):
        step(t)
        return carry

    lax.fori_loop(0, done, body, 0, unroll=unroll)
    for t in range(done, count):
        step(t)


def fill_left(rec, smoothing, left):
    for c in range(rec.shape[0]):
        left[c] = left_operand(rec[c], smoothing[c : c + 1, :])


def by_size(order, starts, run):
    cells = order.shape[0]
    for k, size in enumerate(SIZES):

        def step(n, carry, size=size):
            run(order[n], order[jnp.maximum(n - 1, 0)], order[jnp.minimum(n + 1, cells - 1)], size)
            return carry

        lax.fori_loop(starts[k], starts[k + 1], step, 0)


def density_sums(
    order, starts, partners, groups, table, right, left, square, total, inner_total, value_high, value_low, store
):
    slots = len(groups)

    def product(c, g, size):
        for k, p in enumerate(groups[g]):
            square[k, :size, :] = dot(left[c, :size, :K_ROWS], right[partners[p, c]])

    def reduce():
        ones = jnp.ones((8, HALF), bf16)
        return (dot(ones, value_high[...], LAST) + dot(ones, value_low[...], LAST))[0:1, :]

    def run(c, before, after, size):
        for g, group in enumerate(groups):
            if g == 0:
                store(before, reduce())
            roots = [table[partners[p, c], r : r + 1, :] for p in group for r in (3, 7)]
            doubled = [root + root for root in roots]
            for base in range(0, size, STEP):
                block = pl.ds(base, STEP)
                outer_sum = inner_sum = None
                for k in range(len(roots)):
                    half = slice((k % 2) * HALF, (k % 2 + 1) * HALF)
                    s = jnp.maximum(square[k // 2, block, half], TINY)
                    outer = jnp.maximum(doubled[k] - s * lax.rsqrt(s), 0.0)
                    inner = jnp.maximum(outer - roots[k], 0.0)
                    outer = outer * outer * outer
                    inner = inner * inner * inner
                    outer_sum = outer if k == 0 else outer_sum + outer
                    inner_sum = inner if k == 0 else inner_sum + inner
                if g:
                    outer_sum = total[block, :] + outer_sum
                    inner_sum = inner_total[block, :] + inner_sum
                if g + 1 < slots:
                    total[block, :] = outer_sum
                    inner_total[block, :] = inner_sum
                else:
                    value = 0.25 * outer_sum - inner_sum
                    high = value.astype(bf16)
                    value_high[block, :] = high
                    value_low[block, :] = (value - high.astype(f32)).astype(bf16)
            if g + 1 < slots:
                product(c, g + 1, size)
            else:
                product(after, 0, P_SIZE)

    product(order[0], 0, P_SIZE)
    by_size(order, starts, run)
    store(order[order.shape[0] - 1], reduce())


def near_density_kernel(
    order, starts, partners, rec, rim_lo, rim_hi, smoothing, sums, left, table, right, *scratch
):
    fill_table(table, rec, rim_lo, rim_hi, None, 8)
    fill_left(rec, smoothing, left)

    def step(t):
        right[t] = right_operand(table[t], True)

    for_cells(table.shape[0], step)

    def store(c, row):
        sums[pl.ds(c, 1), :] = row

    density_sums(order, starts, partners, [(0,), (1,)], table, right, left, *scratch, store)


def density_kernel(
    order, starts, partners, counts, send, rec, rim_lo, rim_hi, recv, left, smoothing, energy, near,
    density, press, press_rec, first, last, press_send,
    table, right, sums, *scratch,
):
    cells = rec.shape[0]
    fill_table(table, rec, rim_lo, rim_hi, recv, 8)

    def step(t):
        right[t] = right_operand(table[t], True)

    for_cells(table.shape[0], step)

    def store(c, row):
        sums[pl.ds(c, 1), :] = row

    pairs = partners.shape[0]
    groups = [tuple(range(p, min(p + 2, pairs))) for p in range(NEAR, pairs, 2)]
    density_sums(order, starts, partners, groups, table, right, left, *scratch, store)
    for c in range(cells):
        width = smoothing[c : c + 1, :]
        live = lanes() < counts[c]
        mass = (near[c : c + 1, :] + sums[c : c + 1, :]) * (1.0 / MASS_SCALE)
        rho = mass / (math.pi * width * width * width)
        density[c : c + 1, :] = jnp.where(live, rho, 0.0)
        value = jnp.where(
            live, (adiabatic - 1.0) * energy[c : c + 1, :] / jnp.where(live, rho, 1.0), 0.0
        )
        press[c : c + 1, :] = value
        press_rec[c, 0:1, :] = value[:, :HALF]
        press_rec[c, 1:2, :] = value[:, HALF:]
    first[0] = press_rec[0]
    last[0] = press_rec[cells - 1]
    for v in range(send.shape[1]):
        for k in range(send.shape[0]):
            press_send[v, 2 * k : 2 * k + 2, :] = press_rec[send[k, v]]


def force_sums(
    order, starts, partners, columns, right, left, weights, square, slope_high, slope_low, total, store
):
    count = len(columns)

    def product(c, n, size):
        square[n % 2, :size, :] = dot(left[c, :size, :K_ROWS], right[partners[columns[n], c]])

    def gather(c, n, size):
        w = weights[partners[columns[n], c]]
        return dot(w, slope_high[n % 2, :size, :], LAST) + dot(w, slope_low[n % 2, :size, :], LAST)

    def finish(c):
        found = total[...] + gather(c, count - 1, P_SIZE)
        store(c, found[0:8, :] + found[8:16, :] + found[16:24, :])

    def run(c, before, after, size):
        added = None
        for n in range(count):
            if n + 1 < count:
                product(c, n + 1, size)
            else:
                product(after, 0, P_SIZE)
            if n == 0:
                finish(before)
            else:
                more = gather(c, n - 1, size)
                added = more if n == 1 else added + more
            for base in range(0, size, STEP):
                block = pl.ds(base, STEP)
                s = jnp.minimum(jnp.maximum(square[n % 2, block, :], TINY), 4.0)
                y = lax.rsqrt(s)
                q = s * y
                f = (jnp.minimum(y, 1.0) - 1.0) + (jnp.maximum(q, 1.0) - 0.75 * q)
                high = f.astype(bf16)
                slope_high[n % 2, block, :] = high
                slope_low[n % 2, block, :] = (f - high.astype(f32)).astype(bf16)
        total[:, :size] = added

    product(order[0], 0, P_SIZE)
    by_size(order, starts, run)
    finish(order[order.shape[0] - 1])


def near_force_kernel(
    order, starts, partners, rec, rim_lo, rim_hi, left, press_rec, press_lo, press_hi, sums,
    table, right, press_table, weights, square, slope_high, slope_low, total,
):
    fill_table(table, rec, rim_lo, rim_hi, None, 8)
    fill_table(press_table, press_rec, press_lo, press_hi, None, 2)

    def step(t):
        right[t] = right_operand(table[t], False)
        weights[t] = weight_operand(table[t], press_table[t])

    for_cells(table.shape[0], step)

    def store(c, found):
        sums[c] = found

    force_sums(
        order, starts, partners, list(range(NEAR)), right, left, weights, square, slope_high, slope_low, total, store
    )


def slot_maps(slots, peers):
    block = lax.broadcasted_iota(jnp.int32, (peers, slots), 1) // M
    owner = (block == lax.broadcasted_iota(jnp.int32, (peers, slots), 0)).astype(f32).astype(bf16)
    column = lax.broadcasted_iota(jnp.int32, (slots, HALF), 1)
    slot = lax.broadcasted_iota(jnp.int32, (slots, HALF), 0)
    return owner, column % M == slot % M


def field_map():
    field = lax.broadcasted_iota(jnp.int32, (8, HALF), 1) // M
    return (field == lax.broadcasted_iota(jnp.int32, (8, HALF), 0)).astype(f32)


def force_kernel(
    order, starts, partners, counts, rec, rim_lo, rim_hi, recv, left, press_rec, press_lo, press_hi, press_recv,
    smoothing, pos, vel, press, near, picks,
    state, leaving,
    table, right, press_table, weights, square, slope_high, slope_low, total,
):
    cells = rec.shape[0]
    fill_table(table, rec, rim_lo, rim_hi, recv, 8)
    fill_table(press_table, press_rec, press_lo, press_hi, press_recv, 2)

    def step(t):
        right[t] = right_operand(table[t], False)
        weights[t] = weight_operand(table[t], press_table[t])

    for_cells(table.shape[0], step)

    def store(c, found):
        sums = near[c] + found
        width = smoothing[pl.ds(c, 1), :]
        squared = width * width
        factor = (3.0 * time_step / math.pi) / (squared * squared * width)
        own = press[pl.ds(c, 1), :]
        live = lanes() < counts[c]
        for k in range(3):
            place = pos[k, pl.ds(c, 1), :]
            centred = place - 0.5
            push = own * (centred * sums[3:4, :] - sums[k : k + 1, :]) + (
                centred * sums[7:8, :] - sums[4 + k : 5 + k, :]
            )
            speed = vel[k, pl.ds(c, 1), :] + factor * push
            state[k, pl.ds(c, 1), :] = jnp.where(live, place + time_step * speed, 0.0)
            state[3 + k, pl.ds(c, 1), :] = jnp.where(live, speed, 0.0)

    force_sums(
        order, starts, partners, list(range(NEAR, partners.shape[0])), right, left, weights, square,
        slope_high, slope_low, total, store,
    )

    slots = picks.shape[1]
    picked = picks[...]
    chosen = lax.broadcasted_iota(jnp.int32, (P_SIZE, slots), 0) == picked % P_SIZE
    chosen = chosen.astype(f32).astype(bf16)
    mine = lax.broadcasted_iota(jnp.int32, (cells, slots), 0) == picked // P_SIZE
    parts = [split(state[k]) for k in range(6)]
    parts = jnp.concatenate([part[n] for n in range(3) for part in parts], axis=0).astype(bf16)
    found = dot(parts, chosen)
    rows = []
    for k in range(6):
        value = sum(found[(6 * n + k) * cells : (6 * n + k + 1) * cells, :] for n in range(3))
        rows.append(jnp.sum(jnp.where(mine, value, 0.0), axis=0, keepdims=True))
    found = jnp.concatenate(rows + [jnp.zeros((2, slots), f32)], axis=0)
    owner, same = slot_maps(slots, leaving.shape[0])
    spread = field_map()
    blank = jnp.zeros_like(spread)
    spread = jnp.concatenate(
        [jnp.concatenate([spread if n == k else blank for n in range(3)], axis=1) for k in range(3)], axis=0
    )
    wide = dot(jnp.concatenate(split(found), axis=0).astype(bf16), spread.astype(bf16), FIRST)
    wide = jnp.concatenate(
        [jnp.where(same, wide[:, HALF * n : HALF * (n + 1)], 0.0) for n in range(3)], axis=1
    )
    value = dot(owner, wide.astype(bf16))
    leaving[...] = sum(value[:, HALF * n : HALF * (n + 1)] for n in range(3))


def arrive_kernel(arrived, out):
    owner, same = slot_maps(out.shape[1], arrived.shape[0])
    wide = dot(owner, jnp.concatenate(split(arrived[...]), axis=1).astype(bf16), FIRST)
    wide = jnp.concatenate(
        [jnp.where(same, wide[:, HALF * n : HALF * (n + 1)], 0.0) for n in range(3)], axis=1
    )
    spread = field_map()
    value = dot(jnp.concatenate([spread] * 3, axis=1).astype(bf16), wide.astype(bf16), LAST)
    out[...] = value[: out.shape[0], :]


def call(kernel, outs, smem, vmem, scratch=(), limit=48):
    return pl.pallas_call(
        kernel,
        out_shape=tuple(outs),
        in_specs=[SMEM] * len(smem) + [VMEM] * len(vmem),
        out_specs=tuple(SMEM if out.dtype == jnp.int32 else VMEM for out in outs),
        scratch_shapes=scratch,
        compiler_params=pltpu.CompilerParams(vmem_limit_bytes=limit * 1024 * 1024),
    )(*smem, *vmem)


def to_neighbours(first, last, axis):
    count = lax.axis_size(axis)
    up = [(i, (i + 1) % count) for i in range(count)]
    down = [(j, i) for i, j in up]
    return lax.ppermute(last, axis, up), lax.ppermute(first, axis, down)


def exchange(value):
    return lax.all_to_all(value, "sub", split_axis=0, concat_axis=0, tiled=True)


def on_device(
    positions, velocities, mass, smoothing, energy, cell_counts, send_cells, partners, mig_list, mig_counts
):
    cells = mass.shape[0]
    peers = lax.axis_size("sub")
    kept = send_cells.shape[2]
    near_width = cells + 2
    full_width = near_width + peers * kept
    send = send_cells[0].T
    links = partners.T

    rec, first, last, outgoing, order, starts = call(
        pack_kernel,
        [
            shape(cells, 8, HALF),
            shape(1, 8, HALF),
            shape(1, 8, HALF),
            shape(peers, 8 * kept, HALF),
            jax.ShapeDtypeStruct((cells,), jnp.int32),
            jax.ShapeDtypeStruct((len(SIZES) + 1,), jnp.int32),
        ],
        [cell_counts, send],
        [positions, mass],
        limit=60,
    )
    recv = exchange(outgoing)
    rim_lo, rim_hi = to_neighbours(first, last, "slab")

    keep = jnp.arange(M)[None, :] < mig_counts[0][:, None]
    picks = jnp.where(keep, mig_list[0], -P_SIZE).reshape(1, peers * M)

    def tables(width):
        return [
            pltpu.VMEM((width, 8, HALF), f32),
            pltpu.VMEM((width, K_ROWS, P_SIZE), bf16),
        ]

    def sums(size):
        return [
            pltpu.VMEM((size, P_SIZE, P_SIZE), f32),
            pltpu.VMEM((P_SIZE, HALF), f32),
            pltpu.VMEM((P_SIZE, HALF), f32),
            pltpu.VMEM((P_SIZE, HALF), bf16),
            pltpu.VMEM((P_SIZE, HALF), bf16),
        ]

    near, left = call(
        near_density_kernel,
        [shape(cells, P_SIZE), jax.ShapeDtypeStruct((cells, P_SIZE, HALF), bf16)],
        [order, starts, links],
        [rec, rim_lo, rim_hi, smoothing],
        tables(near_width) + sums(1),
    )
    density, press, press_rec, first, last, press_out = call(
        density_kernel,
        [
            shape(cells, P_SIZE),
            shape(cells, P_SIZE),
            shape(cells, 2, HALF),
            shape(1, 2, HALF),
            shape(1, 2, HALF),
            shape(peers, 2 * kept, HALF),
        ],
        [order, starts, links, cell_counts, send],
        [rec, rim_lo, rim_hi, recv, left, smoothing, energy, near],
        tables(full_width) + [pltpu.VMEM((cells, P_SIZE), f32)] + sums(2),
    )
    press_recv = exchange(press_out)
    press_lo, press_hi = to_neighbours(first, last, "slab")

    def force_tables(width):
        return tables(width) + [
            pltpu.VMEM((width, 2, HALF), f32),
            pltpu.VMEM((width, V_ROWS, P_SIZE), bf16),
            pltpu.VMEM((2, P_SIZE, P_SIZE), f32),
            pltpu.VMEM((2, P_SIZE, P_SIZE), bf16),
            pltpu.VMEM((2, P_SIZE, P_SIZE), bf16),
            pltpu.VMEM((V_ROWS, P_SIZE), f32),
        ]

    (near,) = call(
        near_force_kernel,
        [shape(cells, 8, P_SIZE)],
        [order, starts, links],
        [rec, rim_lo, rim_hi, left, press_rec, press_lo, press_hi],
        force_tables(near_width),
    )
    state, leaving = call(
        force_kernel,
        [shape(6, cells, P_SIZE), shape(peers, HALF)],
        [order, starts, links, cell_counts],
        [
            rec, rim_lo, rim_hi, recv, left, press_rec, press_lo, press_hi, press_recv,
            smoothing, positions, velocities, press, near, picks,
        ],
        force_tables(full_width),
    )
    arrived = exchange(leaving.reshape(peers, 1, HALF)).reshape(peers, HALF)
    (arrivals,) = call(arrive_kernel, [shape(6, peers * M)], [], [arrived])
    return density, state, arrivals


def solution(mesh):
    both = ("slab", "sub")
    return jax.shard_map(
        on_device,
        mesh=mesh,
        in_specs=(
            P(None, both, None),
            P(None, both, None),
            P(both, None),
            P(both, None),
            P(both, None),
            P(both),
            P(both, None, None),
            P(both, None),
            P(both, None, None),
            P(both, None),
        ),
        out_specs=(P(both, None), P(None, both, None), P(None, both)),
        check_vma=False,
    )
```

time: 314 us -> 99.2 us (0.32)
  the two profiles are of different devices: /device:TPU:32 before, /device:TPU:25 now
where the time goes in v2:
time: 99.2 us; the launch traced here: 98.7 us
  Pallas kernels  42.7 us (43%)
  starting transfers between devices  27.2 us (27%)
  blocking collectives  18.1 us (18%)
  waiting for transfers between devices  7.03 us (7%)
  local copies, waits for them, and re-layouts  2.77 us (3%)
    pallas_call x6, Pallas kernels, call(): pl.pallas_call(kernel, out_shape=tuple(outs), in_specs=[SMEM] * len(smem)...  42.7 us
    all_to_all x2, starting transfers between devices, exchange(): return lax.all_to_all(value, 'sub', split_axis=0, concat_axis=0, tiled=True)  23.3 us
    all_to_all x1, blocking collectives, exchange(): return lax.all_to_all(value, 'sub', split_axis=0, concat_axis=0, tiled=True)  18.1 us
    ppermute x4, waiting for transfers between devices, to_neighbours(): return (lax.ppermute(last, axis, up), lax.ppermute(first, axis, down))  7.02 us
    ppermute x4, starting transfers between devices, to_neighbours(): return (lax.ppermute(last, axis, up), lax.ppermute(first, axis, down))  3.88 us
    unnamed x29, local copies, waits for them, and re-layouts  2.58 us
  transfers between devices with their start and end apart: 6, of which 3 were waited for; matrix products, arithmetic and copies ran while one was open for 0% of the time, Pallas kernels for 12%

profile of v2, /device:TPU:25, one launch (start us, length us, event | category | flops | bytes accessed | tf_op | source)
XLA Modules:
  0.0 98.7 jit_solution(8443237208261244469)
XLA Ops:
  0.6 2.1 %shard_map.121 = (f32[16,8,128]{2,1,0:T(8,128)}, f32[1,8,128]{2,1,0:T(8,128)}, f32[1,8,128]{2,1,0:T(8,128)}, f32[32,16,128]{2,1,0:T(8,128)}, s32[16]{0:T(128)}, /*index=5*/s32[10]{0:T(128)}) custom-call(s32[16]{0:T(128)} %counts.5, s32[2,32]{1,0:T(2,128)} %bitcast.15, f32[3,16,256]{2,1,0:T(8,128)} %pos.3, f32[16,256]{1,0:T(8,128)} %mass.1), custom_call_target="tpu_custom_call" | custom-call | tf_op jit(solution)/shard_map/pallas_call | solution.py:472
  2.8 13.0 %all-to-all-start = ((f32[32,16,128]{2,1,0:T(8,128)}), f32[32,16,128]{2,1,0:T(8,128)S(1)}, u32[]{:S(2)}, u32[]{:S(2)}) async-start(f32[32,16,128]{2,1,0:T(8,128)} %get-tuple-element.24), calls=%async_computation | async-start | bytes 524288 | tf_op jit(solution)/shard_map/all_to_all | solution.py:490
  15.8 3.4 %collective-permute-start = (f32[1,8,128]{2,1,0:T(8,128)S(1)}, f32[1,8,128]{2,1,0:T(8,128)S(1)}, u32[]{:S(2)}, u32[]{:S(2)}) collective-permute-start(f32[1,8,128]{2,1,0:T(8,128)S(1)} %copy-done.13), channel_id=1, source_target_pairs={{0,32},{32,64},{64,96},{96,128},{128,160},{160,192},{192,224},{224... | collective-permute-start | bytes 12296 | tf_op jit(solution)/shard_map/ppermute | solution.py:486
  19.2 0.7 copy-done.11
  19.9 0.1 iota_compare_fusion
  19.9 0.1 lt.29
  20.0 0.5 copy-done.10
  20.5 0.1 copy.15
  20.6 0.1 squeeze.7
  20.7 3.0 %collective-permute-done.1.rim_hi = f32[1,8,128]{2,1,0:T(8,128)S(1)} collective-permute-done((f32[1,8,128]{2,1,0:T(8,128)S(1)}, f32[1,8,128]{2,1,0:T(8,128)S(1)}, u32[]{:S(2)}, u32[]{:S(2)}) %collective-permute-start.1) | collective-permute-done | bytes 4128 | tf_op jit(solution)/shard_map/ppermute | solution.py:486
  23.8 0.6 copy-done.6
  24.4 6.0 %shard_map.122 = (f32[16,256]{1,0:T(8,128)S(1)}, bf16[16,256,128]{2,1,0:T(8,128)(2,1)S(1)}) custom-call(s32[16]{0:T(128)S(1)} %copy-done.6, s32[10]{0:T(128)S(1)} %copy-done.7, s32[8,16]{1,0:T(8,128)S(1)} %bitcast.9, f32[16,8,128]{2,1,0:T(8,128)S(1)} %copy-done, f32[1,8,128]{2,1,0:T(8,128)S(1)} %collective-permute-done.rim_lo, ...), custom_call_target="tpu_custom_call" | custom-call | tf_op jit(solution)/shard_map/pallas_call | solution.py:472
  30.3 0.0 copy-start.8
  30.4 0.6 copy-done.8
  31.0 0.0 copy-done.9
  31.1 12.5 %shard_map.123 = (f32[16,256]{1,0:T(8,128)}, f32[16,256]{1,0:T(8,128)S(1)}, f32[16,2,128]{2,1,0:T(2,128)S(1)}, f32[1,2,128]{2,1,0:T(2,128)S(1)}, f32[1,2,128]{2,1,0:T(2,128)S(1)}, /*index=5*/f32[32,4,128]{2,1,0:T(4,128)}) custom-call(s32[16]{0:T(128)S(1)} %copy-done.6, s32[10]{0:T(128)S(1)} %copy-done.7, s32[8,16]{1,0:T(8,128)S(1)} %bitcast.10, ...), custom_call_target="tpu_custom_call" | custom-call | tf_op jit(solution)/shard_map/pallas_call | solution.py:472
  43.5 10.3 %all-to-all-start.1 = ((f32[32,4,128]{2,1,0:T(4,128)}), f32[32,4,128]{2,1,0:T(4,128)S(1)}, u32[]{:S(2)}, u32[]{:S(2)}) async-start(f32[32,4,128]{2,1,0:T(4,128)} %get-tuple-element.31), calls=%async_computation.1 | async-start | bytes 131072 | tf_op jit(solution)/shard_map/all_to_all | solution.py:490
  53.8 0.5 collective-permute-start.3
  54.3 0.6 collective-permute-done.2.press_lo
  55.0 3.4 %collective-permute-done.3.press_hi = f32[1,2,128]{2,1,0:T(2,128)S(1)} collective-permute-done((f32[1,2,128]{2,1,0:T(2,128)S(1)}, f32[1,2,128]{2,1,0:T(2,128)S(1)}, u32[]{:S(2)}, u32[]{:S(2)}) %collective-permute-start.3) | collective-permute-done | bytes 1056 | tf_op jit(solution)/shard_map/ppermute | solution.py:486
  58.4 6.2 %shard_map.124.near = f32[16,8,256]{2,1,0:T(8,128)S(1)} custom-call(s32[16]{0:T(128)S(1)} %copy-done.6, s32[10]{0:T(128)S(1)} %copy-done.7, s32[8,16]{1,0:T(8,128)S(1)} %bitcast.11, f32[16,8,128]{2,1,0:T(8,128)S(1)} %copy-done, f32[1,8,128]{2,1,0:T(8,128)S(1)} %collective-permute-done.rim_lo, f32[1,8,128]{2,1,0:T(8,128)S(1)} %collective-permute-done.1.rim_hi, ...), custom_call_target="tpu_custom_call" | custom-call | tf_op jit(solution)/shard_map/pallas_call | solution.py:472
  64.6 15.0 %shard_map.125 = (f32[6,16,256]{2,1,0:T(8,128)}, f32[32,128]{1,0:T(8,128)S(1)}) custom-call(s32[16]{0:T(128)S(1)} %copy-done.6, s32[10]{0:T(128)S(1)} %copy-done.7, s32[8,16]{1,0:T(8,128)S(1)} %bitcast.12, s32[16]{0:T(128)S(1)} %copy-done.8, f32[16,8,128]{2,1,0:T(8,128)S(1)} %copy-done, f32[1,8,128]{2,1,0:T(8,128)S(1)} %collective-permute-done.rim_lo, ...), custom_call_target="tpu_custom_call" | custom-call | tf_op jit(solution)/shard_map/pallas_call | solution.py:472
  79.6 18.1 %all_to_all.15 = f32[32,1,128]{2,1,0:T(1,128)S(1)} all-to-all(f32[32,1,128]{2,1,0:T(1,128)S(1)} %bitcast.14), channel_id=1, replica_groups=mesh['slab'=16,'sub'=32] {'sub'}, dimensions={0} | all-to-all | bytes 32768 | tf_op jit(solution)/shard_map/all_to_all | solution.py:490
  97.7 1.0 shard_map.126
  (28 shorter events, 0.1 us)
Async XLA Ops:
  2.8 13.1 %copy-start.13 = (f32[1,8,128]{2,1,0:T(8,128)S(1)}, f32[1,8,128]{2,1,0:T(8,128)}, u32[]{:S(2)}) copy-start(f32[1,8,128]{2,1,0:T(8,128)} %get-tuple-element.22) | copy-start | bytes 12292
  2.8 16.4 %copy-start.12 = (f32[1,8,128]{2,1,0:T(8,128)S(1)}, f32[1,8,128]{2,1,0:T(8,128)}, u32[]{:S(2)}) copy-start(f32[1,8,128]{2,1,0:T(8,128)} %get-tuple-element.23) | copy-start | bytes 12292
  2.8 21.0 %copy-start = (f32[16,8,128]{2,1,0:T(8,128)S(1)}, f32[16,8,128]{2,1,0:T(8,128)}, u32[]{:S(2)}) copy-start(f32[16,8,128]{2,1,0:T(8,128)} %get-tuple-element.21.rec) | copy-start | bytes 196612
  2.8 27.5 %all-to-all-start = ((f32[32,16,128]{2,1,0:T(8,128)}), f32[32,16,128]{2,1,0:T(8,128)S(1)}, u32[]{:S(2)}, u32[]{:S(2)}) async-start(f32[32,16,128]{2,1,0:T(8,128)} %get-tuple-element.24), calls=%async_computation | async-start | bytes 524288 | tf_op jit(solution)/shard_map/all_to_all | solution.py:490
  15.8 4.9 %collective-permute-start = (f32[1,8,128]{2,1,0:T(8,128)S(1)}, f32[1,8,128]{2,1,0:T(8,128)S(1)}, u32[]{:S(2)}, u32[]{:S(2)}) collective-permute-start(f32[1,8,128]{2,1,0:T(8,128)S(1)} %copy-done.13), channel_id=1, source_target_pairs={{0,32},{32,64},{64,96},{96,128},{128,160},{160,192},{192,224},{224... | collective-permute-start | bytes 12296 | tf_op jit(solution)/shard_map/ppermute | solution.py:486
  19.2 0.7 copy-start.11
  19.2 4.5 %collective-permute-start.1 = (f32[1,8,128]{2,1,0:T(8,128)S(1)}, f32[1,8,128]{2,1,0:T(8,128)S(1)}, u32[]{:S(2)}, u32[]{:S(2)}) collective-permute-start(f32[1,8,128]{2,1,0:T(8,128)S(1)} %copy-done.12), channel_id=1, source_target_pairs={{32,0},{64,32},{96,64},{128,96},{160,128},{192,160},{224,192},{256... | collective-permute-start | bytes 12296 | tf_op jit(solution)/shard_map/ppermute | solution.py:486
  19.9 0.7 copy-start.10
  20.6 3.1 %copy-start.2 = (f32[16,256]{1,0:T(8,128)S(1)}, f32[16,256]{1,0:T(8,128)}, u32[]{:S(2)}) copy-start(f32[16,256]{1,0:T(8,128)} %smoothing.5) | copy-start | bytes 49156
  20.7 3.0 %copy-start.3 = (s32[16,8]{0,1:T(8,128)S(1)}, s32[16,8]{0,1:T(8,128)}, u32[]{:S(2)}) copy-start(s32[16,8]{0,1:T(8,128)} %param.17) | copy-start | bytes 1540
  23.7 0.6 copy-start.6
  23.7 0.6 copy-start.7
  24.4 6.0 %copy-start.5 = (f32[16,256]{1,0:T(8,128)S(1)}, f32[16,256]{1,0:T(8,128)}, u32[]{:S(2)}) copy-start(f32[16,256]{1,0:T(8,128)} %energy.1) | copy-start | bytes 49156
  30.3 0.7 copy-start.8
  30.4 0.7 copy-start.9
  43.5 21.1 %all-to-all-start.1 = ((f32[32,4,128]{2,1,0:T(4,128)}), f32[32,4,128]{2,1,0:T(4,128)S(1)}, u32[]{:S(2)}, u32[]{:S(2)}) async-start(f32[32,4,128]{2,1,0:T(4,128)} %get-tuple-element.31), calls=%async_computation.1 | async-start | bytes 131072 | tf_op jit(solution)/shard_map/all_to_all | solution.py:490
  53.8 1.2 %collective-permute-start.2 = (f32[1,2,128]{2,1,0:T(2,128)S(1)}, f32[1,2,128]{2,1,0:T(2,128)S(1)}, u32[]{:S(2)}, u32[]{:S(2)}) collective-permute-start(f32[1,2,128]{2,1,0:T(2,128)S(1)} %get-tuple-element.29), channel_id=1, source_target_pairs={{0,32},{32,64},{64,96},{96,128},{128,160},{160,192},{192,224},{224... | collective-permute-start | bytes 3080 | tf_op jit(solution)/shard_map/ppermute | solution.py:486
  53.8 4.5 %collective-permute-start.3 = (f32[1,2,128]{2,1,0:T(2,128)S(1)}, f32[1,2,128]{2,1,0:T(2,128)S(1)}, u32[]{:S(2)}, u32[]{:S(2)}) collective-permute-start(f32[1,2,128]{2,1,0:T(2,128)S(1)} %get-tuple-element.30), channel_id=1, source_target_pairs={{32,0},{64,32},{96,64},{128,96},{160,128},{192,160},{224,192},{256... | collective-permute-start | bytes 3080 | tf_op jit(solution)/shard_map/ppermute | solution.py:486
  58.4 6.2 %copy-start.1 = (f32[3,16,256]{2,1,0:T(8,128)S(1)}, f32[3,16,256]{2,1,0:T(8,128)}, u32[]{:S(2)}) copy-start(f32[3,16,256]{2,1,0:T(8,128)} %pos.3) | copy-start | bytes 147460
  58.4 6.2 %copy-start.4 = (f32[3,16,256]{2,1,0:T(8,128)S(1)}, f32[3,16,256]{2,1,0:T(8,128)}, u32[]{:S(2)}) copy-start(f32[3,16,256]{2,1,0:T(8,128)} %vel.1) | copy-start | bytes 147460

commit v3 on v2

--- a/solution.py
+++ b/solution.py
@@ -26,6 +26,7 @@
 bf16 = jnp.bfloat16
 VMEM = pl.BlockSpec(memory_space=pltpu.VMEM)
 SMEM = pl.BlockSpec(memory_space=pltpu.SMEM)
+HBM = pl.BlockSpec(memory_space=pl.ANY)
 LAST = (((1,), (1,)), ((), ()))
 FIRST = (((0,), (0,)), ((), ()))
 
@@ -51,6 +52,13 @@
 
 def lanes():
     return lax.broadcasted_iota(jnp.int32, (1, P_SIZE), 1)
+
+
+def live_slots(rec):
+    rows = [
+        jnp.concatenate([rec[c, 3:4, :], rec[c, 7:8, :]], axis=1) for c in range(rec.shape[0])
+    ]
+    return jnp.concatenate(rows, axis=0) > 0.0
 
 
 def swap(tile):
@@ -130,23 +138,24 @@
     return jnp.concatenate(parts, axis=1).astype(bf16)
 
 
-def sort_cells(counts, order, starts):
+def sort_cells(counts, order):
     cells = order.shape[0]
-    kinds = [jnp.maximum(lax.div(counts[c] + (STEP - 1), STEP) - SIZES[0] // STEP, 0) for c in range(cells)]
+    keys = []
     for c in range(cells):
-        place = 0
-        for other in range(cells):
-            if other != c:
-                ahead = kinds[other] <= kinds[c] if other < c else kinds[other] < kinds[c]
-                place = place + ahead.astype(jnp.int32)
-        order[place] = jnp.int32(c)
-    for k in range(starts.shape[0]):
-        starts[k] = sum((kind < k).astype(jnp.int32) for kind in kinds)
-
-
-def pack_kernel(counts, send, pos, mass, rec, first, last, out, order, starts):
+        kind = jnp.maximum(lax.div(counts[c] + (STEP - 1), STEP) - SIZES[0] // STEP, 0)
+        keys.append(kind * cells + c)
+    places = [cells - 1 - c for c in range(cells)]
+    for c in range(cells):
+        for other in range(c + 1, cells):
+            behind = (keys[c] > keys[other]).astype(jnp.int32)
+            places[c] = places[c] + (behind - 1)
+            places[other] = places[other] + (1 - behind)
+    for c in range(cells):
+        order[places[c]] = keys[c]
+
+
+def pack_kernel(counts, send, pos, mass, rec, first, last, out):
     cells = mass.shape[0]
-    sort_cells(counts, order, starts)
     scaled = mass[...] * MASS_SCALE
     root = jnp.exp(jnp.log(scaled) * (1.0 / 3.0))
     for _ in range(2):
@@ -196,25 +205,34 @@
         left[c] = left_operand(rec[c], smoothing[c : c + 1, :])
 
 
-def by_size(order, starts, run):
+def cell_at(order, n):
     cells = order.shape[0]
+    return lax.rem(order[jnp.clip(n, 0, cells - 1)], cells)
+
+
+def by_size(order, run):
+    cells = order.shape[0]
+    done = jnp.int32(0)
     for k, size in enumerate(SIZES):
 
-        def step(n, carry, size=size):
-            run(order[n], order[jnp.maximum(n - 1, 0)], order[jnp.minimum(n + 1, cells - 1)], size)
-            return carry
-
-        lax.fori_loop(starts[k], starts[k + 1], step, 0)
+        def more(n, k=k):
+            return (n < cells) & (order[jnp.minimum(n, cells - 1)] < (k + 1) * cells)
+
+        def step(n, size=size):
+            run(cell_at(order, n), cell_at(order, n - 1), cell_at(order, n + 1), size)
+            return n + 1
+
+        done = lax.while_loop(more, step, done)
 
 
 def density_sums(
-    order, starts, partners, groups, table, right, left, square, total, inner_total, value_high, value_low, store
+    order, partners, groups, table, right, left, square, total, inner_total, value_high, value_low, store
 ):
     slots = len(groups)
 
     def product(c, g, size):
         for k, p in enumerate(groups[g]):
-            square[k, :size, :] = dot(left[c, :size, :K_ROWS], right[partners[p, c]])
+            square[k, :size, :] = jnp.maximum(dot(left[c, :size, :K_ROWS], right[partners[p, c]]), TINY)
 
     def reduce():
         ones = jnp.ones((8, HALF), bf16)
@@ -231,7 +249,7 @@
                 outer_sum = inner_sum = None
                 for k in range(len(roots)):
                     half = slice((k % 2) * HALF, (k % 2 + 1) * HALF)
-                    s = jnp.maximum(square[k // 2, block, half], TINY)
+                    s = square[k // 2, block, half]
                     outer = jnp.maximum(doubled[k] - s * lax.rsqrt(s), 0.0)
                     inner = jnp.maximum(outer - roots[k], 0.0)
                     outer = outer * outer * outer
@@ -254,14 +272,25 @@
             else:
                 product(after, 0, P_SIZE)
 
-    product(order[0], 0, P_SIZE)
-    by_size(order, starts, run)
-    store(order[order.shape[0] - 1], reduce())
+    product(cell_at(order, 0), 0, P_SIZE)
+    by_size(order, run)
+    store(cell_at(order, order.shape[0] - 1), reduce())
+
+
+class near_partners:
+    def __init__(self, cells):
+        self.cells = cells
+
+    def __getitem__(self, place):
+        p, c = place
+        return c + 1 if p == 0 else jnp.where(c < self.cells // 2, 0, self.cells + 1)
 
 
 def near_density_kernel(
-    order, starts, partners, rec, rim_lo, rim_hi, smoothing, sums, left, table, right, *scratch
+    counts_ref, rec, rim_lo, rim_hi, smoothing, sums, left, order, table, right, counts, copied, *scratch
 ):
+    copy = pltpu.make_async_copy(counts_ref, counts, copied)
+    copy.start()
     fill_table(table, rec, rim_lo, rim_hi, None, 8)
     fill_left(rec, smoothing, left)
 
@@ -269,19 +298,23 @@
         right[t] = right_operand(table[t], True)
 
     for_cells(table.shape[0], step)
+    copy.wait()
+    sort_cells(counts, order)
 
     def store(c, row):
         sums[pl.ds(c, 1), :] = row
 
-    density_sums(order, starts, partners, [(0,), (1,)], table, right, left, *scratch, store)
+    density_sums(order, near_partners(rec.shape[0]), [(0,), (1,)], table, right, left, *scratch, store)
 
 
 def density_kernel(
-    order, starts, partners, counts, send, rec, rim_lo, rim_hi, recv, left, smoothing, energy, near,
+    order, partners, send_ref, rec, rim_lo, rim_hi, recv, left, smoothing, energy, near,
     density, press, press_rec, first, last, press_send,
-    table, right, sums, *scratch,
+    table, right, sums, send, copied, *scratch,
 ):
     cells = rec.shape[0]
+    copy = pltpu.make_async_copy(send_ref, send, copied)
+    copy.start()
     fill_table(table, rec, rim_lo, rim_hi, recv, 8)
 
     def step(t):
@@ -294,33 +327,33 @@
 
     pairs = partners.shape[0]
     groups = [tuple(range(p, min(p + 2, pairs))) for p in range(NEAR, pairs, 2)]
-    density_sums(order, starts, partners, groups, table, right, left, *scratch, store)
+    density_sums(order, partners, groups, table, right, left, *scratch, store)
+    width = smoothing[...]
+    live = live_slots(rec)
+    rho = (near[...] + sums[...]) * (1.0 / MASS_SCALE) / (math.pi * width * width * width)
+    density[...] = jnp.where(live, rho, 0.0)
+    value = jnp.where(live, (adiabatic - 1.0) * energy[...] / jnp.where(live, rho, 1.0), 0.0)
+    press[...] = value
     for c in range(cells):
-        width = smoothing[c : c + 1, :]
-        live = lanes() < counts[c]
-        mass = (near[c : c + 1, :] + sums[c : c + 1, :]) * (1.0 / MASS_SCALE)
-        rho = mass / (math.pi * width * width * width)
-        density[c : c + 1, :] = jnp.where(live, rho, 0.0)
-        value = jnp.where(
-            live, (adiabatic - 1.0) * energy[c : c + 1, :] / jnp.where(live, rho, 1.0), 0.0
-        )
-        press[c : c + 1, :] = value
-        press_rec[c, 0:1, :] = value[:, :HALF]
-        press_rec[c, 1:2, :] = value[:, HALF:]
+        press_rec[c, 0:1, :] = value[c : c + 1, :HALF]
+        press_rec[c, 1:2, :] = value[c : c + 1, HALF:]
     first[0] = press_rec[0]
     last[0] = press_rec[cells - 1]
+    copy.wait()
     for v in range(send.shape[1]):
         for k in range(send.shape[0]):
             press_send[v, 2 * k : 2 * k + 2, :] = press_rec[send[k, v]]
 
 
 def force_sums(
-    order, starts, partners, columns, right, left, weights, square, slope_high, slope_low, total, store
+    order, partners, columns, right, left, weights, square, slope_high, slope_low, total, store
 ):
     count = len(columns)
+    slots = square.shape[0]
+    ahead = slots - 1
 
     def product(c, n, size):
-        square[n % 2, :size, :] = dot(left[c, :size, :K_ROWS], right[partners[columns[n], c]])
+        square[n % slots, :size, :] = jnp.minimum(jnp.maximum(dot(left[c, :size, :K_ROWS], right[partners[columns[n], c]]), TINY), 4.0)
 
     def gather(c, n, size):
         w = weights[partners[columns[n], c]]
@@ -333,10 +366,10 @@
     def run(c, before, after, size):
         added = None
         for n in range(count):
-            if n + 1 < count:
-                product(c, n + 1, size)
+            if n + ahead < count:
+                product(c, n + ahead, size)
             else:
-                product(after, 0, P_SIZE)
+                product(after, n + ahead - count, P_SIZE)
             if n == 0:
                 finish(before)
             else:
@@ -344,7 +377,7 @@
                 added = more if n == 1 else added + more
             for base in range(0, size, STEP):
                 block = pl.ds(base, STEP)
-                s = jnp.minimum(jnp.maximum(square[n % 2, block, :], TINY), 4.0)
+                s = square[n % slots, block, :]
                 y = lax.rsqrt(s)
                 q = s * y
                 f = (jnp.minimum(y, 1.0) - 1.0) + (jnp.maximum(q, 1.0) - 0.75 * q)
@@ -353,13 +386,14 @@
                 slope_low[n % 2, block, :] = (f - high.astype(f32)).astype(bf16)
         total[:, :size] = added
 
-    product(order[0], 0, P_SIZE)
-    by_size(order, starts, run)
-    finish(order[order.shape[0] - 1])
+    for n in range(ahead):
+        product(cell_at(order, 0), n, P_SIZE)
+    by_size(order, run)
+    finish(cell_at(order, order.shape[0] - 1))
 
 
 def near_force_kernel(
-    order, starts, partners, rec, rim_lo, rim_hi, left, press_rec, press_lo, press_hi, sums,
+    order, rec, rim_lo, rim_hi, left, press_rec, press_lo, press_hi, sums,
     table, right, press_table, weights, square, slope_high, slope_low, total,
 ):
     fill_table(table, rec, rim_lo, rim_hi, None, 8)
@@ -375,7 +409,7 @@
         sums[c] = found
 
     force_sums(
-        order, starts, partners, list(range(NEAR)), right, left, weights, square, slope_high, slope_low, total, store
+        order, near_partners(rec.shape[0]), list(range(NEAR)), right, left, weights, square, slope_high, slope_low, total, store
     )
 
 
@@ -393,10 +427,10 @@
 
 
 def force_kernel(
-    order, starts, partners, counts, rec, rim_lo, rim_hi, recv, left, press_rec, press_lo, press_hi, press_recv,
+    order, partners, rec, rim_lo, rim_hi, recv, left, press_rec, press_lo, press_hi, press_recv,
     smoothing, pos, vel, press, near, picks,
     state, leaving,
-    table, right, press_table, weights, square, slope_high, slope_low, total,
+    table, right, press_table, weights, square, slope_high, slope_low, total, sums,
 ):
     cells = rec.shape[0]
     fill_table(table, rec, rim_lo, rim_hi, recv, 8)
@@ -409,26 +443,27 @@
     for_cells(table.shape[0], step)
 
     def store(c, found):
-        sums = near[c] + found
-        width = smoothing[pl.ds(c, 1), :]
-        squared = width * width
-        factor = (3.0 * time_step / math.pi) / (squared * squared * width)
-        own = press[pl.ds(c, 1), :]
-        live = lanes() < counts[c]
-        for k in range(3):
-            place = pos[k, pl.ds(c, 1), :]
-            centred = place - 0.5
-            push = own * (centred * sums[3:4, :] - sums[k : k + 1, :]) + (
-                centred * sums[7:8, :] - sums[4 + k : 5 + k, :]
-            )
-            speed = vel[k, pl.ds(c, 1), :] + factor * push
-            state[k, pl.ds(c, 1), :] = jnp.where(live, place + time_step * speed, 0.0)
-            state[3 + k, pl.ds(c, 1), :] = jnp.where(live, speed, 0.0)
+        found = near[c] + found
+        for k in range(8):
+            sums[k, pl.ds(c, 1), :] = found[k : k + 1, :]
 
     force_sums(
-        order, starts, partners, list(range(NEAR, partners.shape[0])), right, left, weights, square,
+        order, partners, list(range(NEAR, partners.shape[0])), right, left, weights, square,
         slope_high, slope_low, total, store,
     )
+
+    width = smoothing[...]
+    squared = width * width
+    factor = (3.0 * time_step / math.pi) / (squared * squared * width)
+    own = press[...]
+    live = live_slots(rec)
+    for k in range(3):
+        place = pos[k]
+        centred = place - 0.5
+        push = own * (centred * sums[3] - sums[k]) + (centred * sums[7] - sums[4 + k])
+        speed = vel[k] + factor * push
+        state[k] = jnp.where(live, place + time_step * speed, 0.0)
+        state[3 + k] = jnp.where(live, speed, 0.0)
 
     slots = picks.shape[1]
     picked = picks[...]
@@ -468,15 +503,15 @@
     out[...] = value[: out.shape[0], :]
 
 
-def call(kernel, outs, smem, vmem, scratch=(), limit=48):
+def call(kernel, outs, smem, hbm, vmem, scratch=(), limit=48):
     return pl.pallas_call(
         kernel,
         out_shape=tuple(outs),
-        in_specs=[SMEM] * len(smem) + [VMEM] * len(vmem),
+        in_specs=[SMEM] * len(smem) + [HBM] * len(hbm) + [VMEM] * len(vmem),
         out_specs=tuple(SMEM if out.dtype == jnp.int32 else VMEM for out in outs),
         scratch_shapes=scratch,
         compiler_params=pltpu.CompilerParams(vmem_limit_bytes=limit * 1024 * 1024),
-    )(*smem, *vmem)
+    )(*smem, *hbm, *vmem)
 
 
 def to_neighbours(first, last, axis):
@@ -501,17 +536,16 @@
     send = send_cells[0].T
     links = partners.T
 
-    rec, first, last, outgoing, order, starts = call(
+    rec, first, last, outgoing = call(
         pack_kernel,
         [
             shape(cells, 8, HALF),
             shape(1, 8, HALF),
             shape(1, 8, HALF),
             shape(peers, 8 * kept, HALF),
-            jax.ShapeDtypeStruct((cells,), jnp.int32),
-            jax.ShapeDtypeStruct((len(SIZES) + 1,), jnp.int32),
         ],
         [cell_counts, send],
+        [],
         [positions, mass],
         limit=60,
     )
@@ -536,12 +570,17 @@
             pltpu.VMEM((P_SIZE, HALF), bf16),
         ]
 
-    near, left = call(
+    near, left, order = call(
         near_density_kernel,
-        [shape(cells, P_SIZE), jax.ShapeDtypeStruct((cells, P_SIZE, HALF), bf16)],
-        [order, starts, links],
+        [
+            shape(cells, P_SIZE),
+            jax.ShapeDtypeStruct((cells, P_SIZE, HALF), bf16),
+            jax.ShapeDtypeStruct((cells,), jnp.int32),
+        ],
+        [],
+        [cell_counts],
         [rec, rim_lo, rim_hi, smoothing],
-        tables(near_width) + sums(1),
+        tables(near_width) + [pltpu.SMEM((cells,), jnp.int32), pltpu.SemaphoreType.DMA] + sums(1),
     )
     density, press, press_rec, first, last, press_out = call(
         density_kernel,
@@ -553,18 +592,21 @@
             shape(1, 2, HALF),
             shape(peers, 2 * kept, HALF),
         ],
-        [order, starts, links, cell_counts, send],
+        [order, links],
+        [send],
         [rec, rim_lo, rim_hi, recv, left, smoothing, energy, near],
-        tables(full_width) + [pltpu.VMEM((cells, P_SIZE), f32)] + sums(2),
+        tables(full_width)
+        + [pltpu.VMEM((cells, P_SIZE), f32), pltpu.SMEM((kept, peers), jnp.int32), pltpu.SemaphoreType.DMA]
+        + sums(2),
     )
     press_recv = exchange(press_out)
     press_lo, press_hi = to_neighbours(first, last, "slab")
 
-    def force_tables(width):
+    def force_tables(width, slots):
         return tables(width) + [
             pltpu.VMEM((width, 2, HALF), f32),
             pltpu.VMEM((width, V_ROWS, P_SIZE), bf16),
-            pltpu.VMEM((2, P_SIZE, P_SIZE), f32),
+            pltpu.VMEM((slots, P_SIZE, P_SIZE), f32),
             pltpu.VMEM((2, P_SIZE, P_SIZE), bf16),
             pltpu.VMEM((2, P_SIZE, P_SIZE), bf16),
             pltpu.VMEM((V_ROWS, P_SIZE), f32),
@@ -573,22 +615,24 @@
     (near,) = call(
         near_force_kernel,
         [shape(cells, 8, P_SIZE)],
-        [order, starts, links],
+        [order],
+        [],
         [rec, rim_lo, rim_hi, left, press_rec, press_lo, press_hi],
-        force_tables(near_width),
+        force_tables(near_width, 2),
     )
     state, leaving = call(
         force_kernel,
         [shape(6, cells, P_SIZE), shape(peers, HALF)],
-        [order, starts, links, cell_counts],
+        [order, links],
+        [],
         [
             rec, rim_lo, rim_hi, recv, left, press_rec, press_lo, press_hi, press_recv,
             smoothing, positions, velocities, press, near, picks,
         ],
-        force_tables(full_width),
+        force_tables(full_width, 3) + [pltpu.VMEM((8, cells, P_SIZE), f32)],
     )
     arrived = exchange(leaving.reshape(peers, 1, HALF)).reshape(peers, HALF)
-    (arrivals,) = call(arrive_kernel, [shape(6, peers * M)], [], [arrived])
+    (arrivals,) = call(arrive_kernel, [shape(6, peers * M)], [], [], [arrived])
     return density, state, arrivals
 
 

time: 99.2 us -> 98.3 us (level)
  starting transfers between devices: 27.2 us -> 26.2 us
    unnamed x29 -> x25, local copies, waits for them, and re-layouts: 2.58 us -> 1.94 us
  transfers between devices with their start and end apart: 6 -> 6, of which waited for: 3 -> 3; matrix products, arithmetic and copies ran while one was open for 0% -> 0% of each run, Pallas kernels for 12% -> 13%
where the time goes in v3:
time: 98.3 us; the launch traced here: 97.8 us
  Pallas kernels  43.6 us (44%)
  starting transfers between devices  26.2 us (27%)
  blocking collectives  17.8 us (18%)
  waiting for transfers between devices  7.24 us (7%)
  local copies, waits for them, and re-layouts  2.13 us (2%)
    pallas_call x6, Pallas kernels, call(): pl.pallas_call(kernel, out_shape=tuple(outs), in_specs=[SMEM] * len(smem)...  43.6 us
    all_to_all x2, starting transfers between devices, exchange(): return lax.all_to_all(value, 'sub', split_axis=0, concat_axis=0, tiled=True)  22.3 us
    all_to_all x1, blocking collectives, exchange(): return lax.all_to_all(value, 'sub', split_axis=0, concat_axis=0, tiled=True)  17.8 us
    ppermute x4, waiting for transfers between devices, to_neighbours(): return (lax.ppermute(last, axis, up), lax.ppermute(first, axis, down))  7.23 us
    ppermute x4, starting transfers between devices, to_neighbours(): return (lax.ppermute(last, axis, up), lax.ppermute(first, axis, down))  3.88 us
  transfers between devices with their start and end apart: 6, of which 3 were waited for; matrix products, arithmetic and copies ran while one was open for 0% of the time, Pallas kernels for 13%

profile of v3, /device:TPU:25, one launch (start us, length us, event | category | flops | bytes accessed | tf_op | source)
XLA Modules:
  0.0 97.8 jit_solution(1488195838154539983)
XLA Ops:
  0.6 1.7 %shard_map.121 = (f32[16,8,128]{2,1,0:T(8,128)}, f32[1,8,128]{2,1,0:T(8,128)}, f32[1,8,128]{2,1,0:T(8,128)}, f32[32,16,128]{2,1,0:T(8,128)}) custom-call(s32[16]{0:T(128)} %counts_ref.1, s32[2,32]{1,0:T(2,128)} %bitcast.13, f32[3,16,256]{2,1,0:T(8,128)} %pos.3, f32[16,256]{1,0:T(8,128)} %mass.1), custom_call_target="tpu_custom_call" | custom-call | tf_op jit(solution)/shard_map/pallas_call | solution.py:507
  2.3 13.0 %all-to-all-start = ((f32[32,16,128]{2,1,0:T(8,128)}), f32[32,16,128]{2,1,0:T(8,128)S(1)}, u32[]{:S(2)}, u32[]{:S(2)}) async-start(f32[32,16,128]{2,1,0:T(8,128)} %get-tuple-element.22), calls=%async_computation | async-start | bytes 524288 | tf_op jit(solution)/shard_map/all_to_all | solution.py:525
  15.3 3.4 %collective-permute-start = (f32[1,8,128]{2,1,0:T(8,128)S(1)}, f32[1,8,128]{2,1,0:T(8,128)S(1)}, u32[]{:S(2)}, u32[]{:S(2)}) collective-permute-start(f32[1,8,128]{2,1,0:T(8,128)S(1)} %copy-done.11), channel_id=1, source_target_pairs={{0,32},{32,64},{64,96},{96,128},{128,160},{160,192},{192,224},{224... | collective-permute-start | bytes 12296 | tf_op jit(solution)/shard_map/ppermute | solution.py:521
  18.7 0.7 copy-done.9
  19.4 0.1 iota_compare_fusion
  19.4 0.1 lt.29
  19.5 0.5 copy-done.8
  20.1 0.1 copy.15
  20.1 0.1 squeeze.7
  20.2 0.0 copy-start.7
  20.2 3.0 %collective-permute-done.1.rim_hi = f32[1,8,128]{2,1,0:T(8,128)S(1)} collective-permute-done((f32[1,8,128]{2,1,0:T(8,128)S(1)}, f32[1,8,128]{2,1,0:T(8,128)S(1)}, u32[]{:S(2)}, u32[]{:S(2)}) %collective-permute-start.1) | collective-permute-done | bytes 4128 | tf_op jit(solution)/shard_map/ppermute | solution.py:521
  23.3 6.6 %shard_map.122 = (f32[16,256]{1,0:T(8,128)S(1)}, bf16[16,256,128]{2,1,0:T(8,128)(2,1)S(1)}, s32[16]{0:T(128)S(1)}) custom-call(s32[16]{0:T(128)S(1)} %copy-done.7, f32[16,8,128]{2,1,0:T(8,128)S(1)} %copy-done, f32[1,8,128]{2,1,0:T(8,128)S(1)} %collective-permute-done.rim_lo, f32[1,8,128]{2,1,0:T(8,128)S(1)} %collective-permute-done.1.rim_hi, ...), custom_call_target="tpu_custom_call" | custom-call | tf_op jit(solution)/shard_map/pallas_call | solution.py:507
  29.9 0.6 copy-done.5
  30.5 0.0 copy-done.6
  30.6 12.9 %shard_map.123 = (f32[16,256]{1,0:T(8,128)}, f32[16,256]{1,0:T(8,128)S(1)}, f32[16,2,128]{2,1,0:T(2,128)S(1)}, f32[1,2,128]{2,1,0:T(2,128)S(1)}, f32[1,2,128]{2,1,0:T(2,128)S(1)}, /*index=5*/f32[32,4,128]{2,1,0:T(4,128)}) custom-call(s32[16]{0:T(128)S(1)} %get-tuple-element.21.order, s32[8,16]{1,0:T(8,128)S(1)} %bitcast.10, s32[2,32]{1,0:T(2,128)S(1)} %bitcast.14, ...), custom_call_target="tpu_custom_call" | custom-call | tf_op jit(solution)/shard_map/pallas_call | solution.py:507
  43.5 9.3 %all-to-all-start.1 = ((f32[32,4,128]{2,1,0:T(4,128)}), f32[32,4,128]{2,1,0:T(4,128)S(1)}, u32[]{:S(2)}, u32[]{:S(2)}) async-start(f32[32,4,128]{2,1,0:T(4,128)} %get-tuple-element.29), calls=%async_computation.1 | async-start | bytes 131072 | tf_op jit(solution)/shard_map/all_to_all | solution.py:525
  52.8 0.2 collective-permute-start.2
  53.0 0.3 collective-permute-start.3
  53.3 0.6 collective-permute-done.2.press_lo
  53.9 3.6 %collective-permute-done.3.press_hi = f32[1,2,128]{2,1,0:T(2,128)S(1)} collective-permute-done((f32[1,2,128]{2,1,0:T(2,128)S(1)}, f32[1,2,128]{2,1,0:T(2,128)S(1)}, u32[]{:S(2)}, u32[]{:S(2)}) %collective-permute-start.3) | collective-permute-done | bytes 1056 | tf_op jit(solution)/shard_map/ppermute | solution.py:521
  57.5 6.3 %shard_map.124.near = f32[16,8,256]{2,1,0:T(8,128)S(1)} custom-call(s32[16]{0:T(128)S(1)} %get-tuple-element.21.order, f32[16,8,128]{2,1,0:T(8,128)S(1)} %copy-done, f32[1,8,128]{2,1,0:T(8,128)S(1)} %collective-permute-done.rim_lo, f32[1,8,128]{2,1,0:T(8,128)S(1)} %collective-permute-done.1.rim_hi, bf16[16,256,128]{2,1,0:T(8,128)(2,1)S(1)} %get-tuple-element.23.left, ...), custom_call_target="tpu_custom_call" | custom-call | tf_op jit(solution)/shard_map/pallas_call | solution.py:507
  63.8 15.2 %shard_map.125 = (f32[6,16,256]{2,1,0:T(8,128)}, f32[32,128]{1,0:T(8,128)S(1)}) custom-call(s32[16]{0:T(128)S(1)} %get-tuple-element.21.order, s32[8,16]{1,0:T(8,128)S(1)} %bitcast.11, f32[16,8,128]{2,1,0:T(8,128)S(1)} %copy-done, f32[1,8,128]{2,1,0:T(8,128)S(1)} %collective-permute-done.rim_lo, f32[1,8,128]{2,1,0:T(8,128)S(1)} %collective-permute-done.1.rim_hi, ...), custom_call_target="tpu_custom_call" | custom-call | tf_op jit(solution)/shard_map/pallas_call | solution.py:507
  79.0 17.8 %all_to_all.15 = f32[32,1,128]{2,1,0:T(1,128)S(1)} all-to-all(f32[32,1,128]{2,1,0:T(1,128)S(1)} %bitcast.12), channel_id=1, replica_groups=mesh['slab'=16,'sub'=32] {'sub'}, dimensions={0} | all-to-all | bytes 32768 | tf_op jit(solution)/shard_map/all_to_all | solution.py:525
  96.9 1.0 shard_map.126
  (24 shorter events, 0.1 us)
Async XLA Ops:
  2.3 13.1 %copy-start.11 = (f32[1,8,128]{2,1,0:T(8,128)S(1)}, f32[1,8,128]{2,1,0:T(8,128)}, u32[]{:S(2)}) copy-start(f32[1,8,128]{2,1,0:T(8,128)} %get-tuple-element.19) | copy-start | bytes 12292
  2.3 16.4 %copy-start.10 = (f32[1,8,128]{2,1,0:T(8,128)S(1)}, f32[1,8,128]{2,1,0:T(8,128)}, u32[]{:S(2)}) copy-start(f32[1,8,128]{2,1,0:T(8,128)} %get-tuple-element.20) | copy-start | bytes 12292
  2.3 21.0 %copy-start = (f32[16,8,128]{2,1,0:T(8,128)S(1)}, f32[16,8,128]{2,1,0:T(8,128)}, u32[]{:S(2)}) copy-start(f32[16,8,128]{2,1,0:T(8,128)} %get-tuple-element.18.rec) | copy-start | bytes 196612
  2.3 27.6 %all-to-all-start = ((f32[32,16,128]{2,1,0:T(8,128)}), f32[32,16,128]{2,1,0:T(8,128)S(1)}, u32[]{:S(2)}, u32[]{:S(2)}) async-start(f32[32,16,128]{2,1,0:T(8,128)} %get-tuple-element.22), calls=%async_computation | async-start | bytes 524288 | tf_op jit(solution)/shard_map/all_to_all | solution.py:525
  15.3 4.9 %collective-permute-start = (f32[1,8,128]{2,1,0:T(8,128)S(1)}, f32[1,8,128]{2,1,0:T(8,128)S(1)}, u32[]{:S(2)}, u32[]{:S(2)}) collective-permute-start(f32[1,8,128]{2,1,0:T(8,128)S(1)} %copy-done.11), channel_id=1, source_target_pairs={{0,32},{32,64},{64,96},{96,128},{128,160},{160,192},{192,224},{224... | collective-permute-start | bytes 12296 | tf_op jit(solution)/shard_map/ppermute | solution.py:521
  18.7 0.7 copy-start.9
  18.7 4.5 %collective-permute-start.1 = (f32[1,8,128]{2,1,0:T(8,128)S(1)}, f32[1,8,128]{2,1,0:T(8,128)S(1)}, u32[]{:S(2)}, u32[]{:S(2)}) collective-permute-start(f32[1,8,128]{2,1,0:T(8,128)S(1)} %copy-done.10), channel_id=1, source_target_pairs={{32,0},{64,32},{96,64},{128,96},{160,128},{192,160},{224,192},{256... | collective-permute-start | bytes 12296 | tf_op jit(solution)/shard_map/ppermute | solution.py:521
  19.4 0.7 copy-start.8
  20.1 3.2 %copy-start.2 = (f32[16,256]{1,0:T(8,128)S(1)}, f32[16,256]{1,0:T(8,128)}, u32[]{:S(2)}) copy-start(f32[16,256]{1,0:T(8,128)} %smoothing.5) | copy-start | bytes 49156
  20.2 3.0 %copy-start.7 = (s32[16]{0:T(128)S(1)}, s32[16]{0:T(128)}, u32[]{:S(2)}) copy-start(s32[16]{0:T(128)} %counts_ref.1) | copy-start | bytes 196
  23.3 6.6 %copy-start.4 = (f32[16,256]{1,0:T(8,128)S(1)}, f32[16,256]{1,0:T(8,128)}, u32[]{:S(2)}) copy-start(f32[16,256]{1,0:T(8,128)} %energy.1) | copy-start | bytes 49156
  29.8 0.7 copy-start.5
  29.9 0.7 copy-start.6
  43.5 20.3 %all-to-all-start.1 = ((f32[32,4,128]{2,1,0:T(4,128)}), f32[32,4,128]{2,1,0:T(4,128)S(1)}, u32[]{:S(2)}, u32[]{:S(2)}) async-start(f32[32,4,128]{2,1,0:T(4,128)} %get-tuple-element.29), calls=%async_computation.1 | async-start | bytes 131072 | tf_op jit(solution)/shard_map/all_to_all | solution.py:525
  52.8 1.2 %collective-permute-start.2 = (f32[1,2,128]{2,1,0:T(2,128)S(1)}, f32[1,2,128]{2,1,0:T(2,128)S(1)}, u32[]{:S(2)}, u32[]{:S(2)}) collective-permute-start(f32[1,2,128]{2,1,0:T(2,128)S(1)} %get-tuple-element.27), channel_id=1, source_target_pairs={{0,32},{32,64},{64,96},{96,128},{128,160},{160,192},{192,224},{224... | collective-permute-start | bytes 3080 | tf_op jit(solution)/shard_map/ppermute | solution.py:521
  53.0 4.5 %collective-permute-start.3 = (f32[1,2,128]{2,1,0:T(2,128)S(1)}, f32[1,2,128]{2,1,0:T(2,128)S(1)}, u32[]{:S(2)}, u32[]{:S(2)}) collective-permute-start(f32[1,2,128]{2,1,0:T(2,128)S(1)} %get-tuple-element.28), channel_id=1, source_target_pairs={{32,0},{64,32},{96,64},{128,96},{160,128},{192,160},{224,192},{256... | collective-permute-start | bytes 3080 | tf_op jit(solution)/shard_map/ppermute | solution.py:521
  57.5 6.3 %copy-start.1 = (f32[3,16,256]{2,1,0:T(8,128)S(1)}, f32[3,16,256]{2,1,0:T(8,128)}, u32[]{:S(2)}) copy-start(f32[3,16,256]{2,1,0:T(8,128)} %pos.3) | copy-start | bytes 147460
  57.5 6.3 %copy-start.3 = (f32[3,16,256]{2,1,0:T(8,128)S(1)}, f32[3,16,256]{2,1,0:T(8,128)}, u32[]{:S(2)}) copy-start(f32[3,16,256]{2,1,0:T(8,128)} %vel.1) | copy-start | bytes 147460

commit v4 on v3

--- a/solution.py
+++ b/solution.py
@@ -277,6 +277,18 @@
     store(cell_at(order, order.shape[0] - 1), reduce())
 
 
+def begin(*copies):
+    started = [pltpu.make_async_copy(*copy) for copy in copies]
+    for copy in started:
+        copy.start()
+    return started
+
+
+def finish_all(started):
+    for copy in started:
+        copy.wait()
+
+
 class near_partners:
     def __init__(self, cells):
         self.cells = cells
@@ -308,19 +320,21 @@
 
 
 def density_kernel(
-    order, partners, send_ref, rec, rim_lo, rim_hi, recv, left, smoothing, energy, near,
-    density, press, press_rec, first, last, press_send,
-    table, right, sums, send, copied, *scratch,
+    order_ref, partners_ref, send_ref, rec, rim_lo, rim_hi, recv, left, smoothing, energy, near,
+    density_ref, press, press_rec, first, last, press_send,
+    table, right, sums, density, order, partners, send, copied, *scratch,
 ):
     cells = rec.shape[0]
-    copy = pltpu.make_async_copy(send_ref, send, copied)
-    copy.start()
+    lists = begin(
+        (order_ref, order, copied.at[0]), (partners_ref, partners, copied.at[1]), (send_ref, send, copied.at[2])
+    )
     fill_table(table, rec, rim_lo, rim_hi, recv, 8)
 
     def step(t):
         right[t] = right_operand(table[t], True)
 
     for_cells(table.shape[0], step)
+    finish_all(lists)
 
     def store(c, row):
         sums[pl.ds(c, 1), :] = row
@@ -332,6 +346,7 @@
     live = live_slots(rec)
     rho = (near[...] + sums[...]) * (1.0 / MASS_SCALE) / (math.pi * width * width * width)
     density[...] = jnp.where(live, rho, 0.0)
+    stored = begin((density, density_ref, copied.at[3]))
     value = jnp.where(live, (adiabatic - 1.0) * energy[...] / jnp.where(live, rho, 1.0), 0.0)
     press[...] = value
     for c in range(cells):
@@ -339,10 +354,10 @@
         press_rec[c, 1:2, :] = value[c : c + 1, HALF:]
     first[0] = press_rec[0]
     last[0] = press_rec[cells - 1]
-    copy.wait()
     for v in range(send.shape[1]):
         for k in range(send.shape[0]):
             press_send[v, 2 * k : 2 * k + 2, :] = press_rec[send[k, v]]
+    finish_all(stored)
 
 
 def force_sums(
@@ -393,9 +408,10 @@
 
 
 def near_force_kernel(
-    order, rec, rim_lo, rim_hi, left, press_rec, press_lo, press_hi, sums,
-    table, right, press_table, weights, square, slope_high, slope_low, total,
+    order_ref, rec, rim_lo, rim_hi, left, press_rec, press_lo, press_hi, sums,
+    order, copied, table, right, press_table, weights, square, slope_high, slope_low, total,
 ):
+    lists = begin((order_ref, order, copied.at[0]))
     fill_table(table, rec, rim_lo, rim_hi, None, 8)
     fill_table(press_table, press_rec, press_lo, press_hi, None, 2)
 
@@ -404,6 +420,7 @@
         weights[t] = weight_operand(table[t], press_table[t])
 
     for_cells(table.shape[0], step)
+    finish_all(lists)
 
     def store(c, found):
         sums[c] = found
@@ -427,12 +444,13 @@
 
 
 def force_kernel(
-    order, partners, rec, rim_lo, rim_hi, recv, left, press_rec, press_lo, press_hi, press_recv,
+    order_ref, partners_ref, rec, rim_lo, rim_hi, recv, left, press_rec, press_lo, press_hi, press_recv,
     smoothing, pos, vel, press, near, picks,
-    state, leaving,
-    table, right, press_table, weights, square, slope_high, slope_low, total, sums,
+    state_ref, leaving,
+    state, order, partners, copied, table, right, press_table, weights, square, slope_high, slope_low, total, sums,
 ):
     cells = rec.shape[0]
+    lists = begin((order_ref, order, copied.at[0]), (partners_ref, partners, copied.at[1]))
     fill_table(table, rec, rim_lo, rim_hi, recv, 8)
     fill_table(press_table, press_rec, press_lo, press_hi, press_recv, 2)
 
@@ -441,6 +459,7 @@
         weights[t] = weight_operand(table[t], press_table[t])
 
     for_cells(table.shape[0], step)
+    finish_all(lists)
 
     def store(c, found):
         found = near[c] + found
@@ -465,6 +484,7 @@
         state[k] = jnp.where(live, place + time_step * speed, 0.0)
         state[3 + k] = jnp.where(live, speed, 0.0)
 
+    stored = begin((state, state_ref, copied.at[2]))
     slots = picks.shape[1]
     picked = picks[...]
     chosen = lax.broadcasted_iota(jnp.int32, (P_SIZE, slots), 0) == picked % P_SIZE
@@ -490,6 +510,7 @@
     )
     value = dot(owner, wide.astype(bf16))
     leaving[...] = sum(value[:, HALF * n : HALF * (n + 1)] for n in range(3))
+    finish_all(stored)
 
 
 def arrive_kernel(arrived, out):
@@ -503,12 +524,14 @@
     out[...] = value[: out.shape[0], :]
 
 
-def call(kernel, outs, smem, hbm, vmem, scratch=(), limit=48):
+def call(kernel, outs, smem, hbm, vmem, scratch=(), limit=48, direct=()):
     return pl.pallas_call(
         kernel,
         out_shape=tuple(outs),
         in_specs=[SMEM] * len(smem) + [HBM] * len(hbm) + [VMEM] * len(vmem),
-        out_specs=tuple(SMEM if out.dtype == jnp.int32 else VMEM for out in outs),
+        out_specs=tuple(
+            HBM if n in direct else SMEM if out.dtype == jnp.int32 else VMEM for n, out in enumerate(outs)
+        ),
         scratch_shapes=scratch,
         compiler_params=pltpu.CompilerParams(vmem_limit_bytes=limit * 1024 * 1024),
     )(*smem, *hbm, *vmem)
@@ -592,12 +615,15 @@
             shape(1, 2, HALF),
             shape(peers, 2 * kept, HALF),
         ],
-        [order, links],
-        [send],
+        [],
+        [order, links, send],
         [rec, rim_lo, rim_hi, recv, left, smoothing, energy, near],
         tables(full_width)
-        + [pltpu.VMEM((cells, P_SIZE), f32), pltpu.SMEM((kept, peers), jnp.int32), pltpu.SemaphoreType.DMA]
+        + [pltpu.VMEM((cells, P_SIZE), f32), pltpu.VMEM((cells, P_SIZE), f32)]
+        + [pltpu.SMEM((cells,), jnp.int32), pltpu.SMEM(links.shape, jnp.int32), pltpu.SMEM(send.shape, jnp.int32)]
+        + [pltpu.SemaphoreType.DMA((4,))]
         + sums(2),
+        direct=(0,),
     )
     press_recv = exchange(press_out)
     press_lo, press_hi = to_neighbours(first, last, "slab")
@@ -615,21 +641,25 @@
     (near,) = call(
         near_force_kernel,
         [shape(cells, 8, P_SIZE)],
+        [],
         [order],
-        [],
         [rec, rim_lo, rim_hi, left, press_rec, press_lo, press_hi],
-        force_tables(near_width, 2),
+        [pltpu.SMEM((cells,), jnp.int32), pltpu.SemaphoreType.DMA((1,))] + force_tables(near_width, 2),
     )
     state, leaving = call(
         force_kernel,
         [shape(6, cells, P_SIZE), shape(peers, HALF)],
+        [],
         [order, links],
-        [],
         [
             rec, rim_lo, rim_hi, recv, left, press_rec, press_lo, press_hi, press_recv,
             smoothing, positions, velocities, press, near, picks,
         ],
-        force_tables(full_width, 3) + [pltpu.VMEM((8, cells, P_SIZE), f32)],
+        [pltpu.VMEM((6, cells, P_SIZE), f32), pltpu.SMEM((cells,), jnp.int32), pltpu.SMEM(links.shape, jnp.int32)]
+        + [pltpu.SemaphoreType.DMA((3,))]
+        + force_tables(full_width, 3)
+        + [pltpu.VMEM((8, cells, P_SIZE), f32)],
+        direct=(0,),
     )
     arrived = exchange(leaving.reshape(peers, 1, HALF)).reshape(peers, HALF)
     (arrivals,) = call(arrive_kernel, [shape(6, peers * M)], [], [], [arrived])

time: 98.3 us -> 98.3 us (level)
  no operation moved by 1% of the time
where the time goes in v4:
time: 98.3 us; the launch traced here: 98.7 us
  Pallas kernels  44.3 us (45%)
  starting transfers between devices  26.6 us (27%)
  blocking collectives  17.8 us (18%)
  waiting for transfers between devices  7.02 us (7%)
  local copies, waits for them, and re-layouts  2.13 us (2%)
    pallas_call x6, Pallas kernels, call(): pl.pallas_call(kernel, out_shape=tuple(outs), in_specs=[SMEM] * len(smem)...  44.3 us
    all_to_all x2, starting transfers between devices, exchange(): return lax.all_to_all(value, 'sub', split_axis=0, concat_axis=0, tiled=True)  22.7 us
    all_to_all x1, blocking collectives, exchange(): return lax.all_to_all(value, 'sub', split_axis=0, concat_axis=0, tiled=True)  17.8 us
    ppermute x4, waiting for transfers between devices, to_neighbours(): return (lax.ppermute(last, axis, up), lax.ppermute(first, axis, down))  7.02 us
    ppermute x4, starting transfers between devices, to_neighbours(): return (lax.ppermute(last, axis, up), lax.ppermute(first, axis, down))  3.88 us
  transfers between devices with their start and end apart: 6, of which 3 were waited for; matrix products, arithmetic and copies ran while one was open for 0% of the time, Pallas kernels for 13%

profile of v4, /device:TPU:25, one launch (start us, length us, event | category | flops | bytes accessed | tf_op | source)
XLA Modules:
  0.0 98.7 jit_solution(4830037366330299857)
XLA Ops:
  0.6 1.7 %shard_map.121 = (f32[16,8,128]{2,1,0:T(8,128)}, f32[1,8,128]{2,1,0:T(8,128)}, f32[1,8,128]{2,1,0:T(8,128)}, f32[32,16,128]{2,1,0:T(8,128)}) custom-call(s32[16]{0:T(128)} %counts_ref.1, s32[2,32]{1,0:T(2,128)} %bitcast.13, f32[3,16,256]{2,1,0:T(8,128)} %pos.3, f32[16,256]{1,0:T(8,128)} %mass.1), custom_call_target="tpu_custom_call" | custom-call | tf_op jit(solution)/shard_map/pallas_call | solution.py:528
  2.3 13.0 %all-to-all-start = ((f32[32,16,128]{2,1,0:T(8,128)}), f32[32,16,128]{2,1,0:T(8,128)S(1)}, u32[]{:S(2)}, u32[]{:S(2)}) async-start(f32[32,16,128]{2,1,0:T(8,128)} %get-tuple-element.22), calls=%async_computation | async-start | bytes 524288 | tf_op jit(solution)/shard_map/all_to_all | solution.py:548
  15.3 3.4 %collective-permute-start = (f32[1,8,128]{2,1,0:T(8,128)S(1)}, f32[1,8,128]{2,1,0:T(8,128)S(1)}, u32[]{:S(2)}, u32[]{:S(2)}) collective-permute-start(f32[1,8,128]{2,1,0:T(8,128)S(1)} %copy-done.11), channel_id=1, source_target_pairs={{0,32},{32,64},{64,96},{96,128},{128,160},{160,192},{192,224},{224... | collective-permute-start | bytes 12296 | tf_op jit(solution)/shard_map/ppermute | solution.py:544
  18.7 0.7 copy-done.9
  19.4 0.1 iota_compare_fusion
  19.4 0.1 lt.29
  19.5 0.5 copy-done.8
  20.1 0.1 copy.15
  20.1 0.1 squeeze.7
  20.2 0.0 copy-start.7
  20.2 3.0 %collective-permute-done.1.rim_hi = f32[1,8,128]{2,1,0:T(8,128)S(1)} collective-permute-done((f32[1,8,128]{2,1,0:T(8,128)S(1)}, f32[1,8,128]{2,1,0:T(8,128)S(1)}, u32[]{:S(2)}, u32[]{:S(2)}) %collective-permute-start.1) | collective-permute-done | bytes 4128 | tf_op jit(solution)/shard_map/ppermute | solution.py:544
  23.3 6.7 %shard_map.122 = (f32[16,256]{1,0:T(8,128)S(1)}, bf16[16,256,128]{2,1,0:T(8,128)(2,1)S(1)}, s32[16]{0:T(128)S(1)}) custom-call(s32[16]{0:T(128)S(1)} %copy-done.7, f32[16,8,128]{2,1,0:T(8,128)S(1)} %copy-done, f32[1,8,128]{2,1,0:T(8,128)S(1)} %collective-permute-done.rim_lo, f32[1,8,128]{2,1,0:T(8,128)S(1)} %collective-permute-done.1.rim_hi, ...), custom_call_target="tpu_custom_call" | custom-call | tf_op jit(solution)/shard_map/pallas_call | solution.py:528
  30.0 0.6 copy-done.5
  30.7 0.0 copy-done.6
  30.7 13.5 %shard_map.123 = (f32[16,256]{1,0:T(8,128)}, f32[16,256]{1,0:T(8,128)S(1)}, f32[16,2,128]{2,1,0:T(2,128)S(1)}, f32[1,2,128]{2,1,0:T(2,128)S(1)}, f32[1,2,128]{2,1,0:T(2,128)S(1)}, /*index=5*/f32[32,4,128]{2,1,0:T(4,128)}) custom-call(s32[16]{0:T(128)S(1)} %get-tuple-element.21.order_ref, s32[8,16]{1,0:T(8,128)S(1)} %bitcast.10, s32[2,32]{1,0:T(2,128)S(1)} %bitcast.14, ...), custom_call_target="tpu_custom_call" | custom-call | tf_op jit(solution)/shard_map/pallas_call | solution.py:528
  44.2 9.7 %all-to-all-start.1 = ((f32[32,4,128]{2,1,0:T(4,128)}), f32[32,4,128]{2,1,0:T(4,128)S(1)}, u32[]{:S(2)}, u32[]{:S(2)}) async-start(f32[32,4,128]{2,1,0:T(4,128)} %get-tuple-element.29), calls=%async_computation.1 | async-start | bytes 131072 | tf_op jit(solution)/shard_map/all_to_all | solution.py:548
  53.9 0.0 collective-permute-start.2
  53.9 0.5 collective-permute-start.3
  54.4 0.6 collective-permute-done.2.press_lo
  55.0 3.4 %collective-permute-done.3.press_hi = f32[1,2,128]{2,1,0:T(2,128)S(1)} collective-permute-done((f32[1,2,128]{2,1,0:T(2,128)S(1)}, f32[1,2,128]{2,1,0:T(2,128)S(1)}, u32[]{:S(2)}, u32[]{:S(2)}) %collective-permute-start.3) | collective-permute-done | bytes 1056 | tf_op jit(solution)/shard_map/ppermute | solution.py:544
  58.4 6.1 %shard_map.124.near = f32[16,8,256]{2,1,0:T(8,128)S(1)} custom-call(s32[16]{0:T(128)S(1)} %get-tuple-element.21.order_ref, f32[16,8,128]{2,1,0:T(8,128)S(1)} %copy-done, f32[1,8,128]{2,1,0:T(8,128)S(1)} %collective-permute-done.rim_lo, f32[1,8,128]{2,1,0:T(8,128)S(1)} %collective-permute-done.1.rim_hi, bf16[16,256,128]{2,1,0:T(8,128)(2,1)S(1)} %get-tuple-element.23.left, ...), custom_call_target="tpu_custom_call" | custom-call | tf_op jit(solution)/shard_map/pallas_call | solution.py:528
  64.6 15.3 %shard_map.125 = (f32[6,16,256]{2,1,0:T(8,128)}, f32[32,128]{1,0:T(8,128)S(1)}) custom-call(s32[16]{0:T(128)S(1)} %get-tuple-element.21.order_ref, s32[8,16]{1,0:T(8,128)S(1)} %bitcast.11, f32[16,8,128]{2,1,0:T(8,128)S(1)} %copy-done, f32[1,8,128]{2,1,0:T(8,128)S(1)} %collective-permute-done.rim_lo, f32[1,8,128]{2,1,0:T(8,128)S(1)} %collective-permute-done.1.rim_hi, ...), custom_call_target="tpu_custom_call" | custom-call | tf_op jit(solution)/shard_map/pallas_call | solution.py:528
  79.9 17.8 %all_to_all.15 = f32[32,1,128]{2,1,0:T(1,128)S(1)} all-to-all(f32[32,1,128]{2,1,0:T(1,128)S(1)} %bitcast.12), channel_id=1, replica_groups=mesh['slab'=16,'sub'=32] {'sub'}, dimensions={0} | all-to-all | bytes 32768 | tf_op jit(solution)/shard_map/all_to_all | solution.py:548
  97.7 1.0 shard_map.126
  (24 shorter events, 0.1 us)
Async XLA Ops:
  2.3 13.1 %copy-start.11 = (f32[1,8,128]{2,1,0:T(8,128)S(1)}, f32[1,8,128]{2,1,0:T(8,128)}, u32[]{:S(2)}) copy-start(f32[1,8,128]{2,1,0:T(8,128)} %get-tuple-element.19) | copy-start | bytes 12292
  2.3 16.4 %copy-start.10 = (f32[1,8,128]{2,1,0:T(8,128)S(1)}, f32[1,8,128]{2,1,0:T(8,128)}, u32[]{:S(2)}) copy-start(f32[1,8,128]{2,1,0:T(8,128)} %get-tuple-element.20) | copy-start | bytes 12292
  2.3 21.0 %copy-start = (f32[16,8,128]{2,1,0:T(8,128)S(1)}, f32[16,8,128]{2,1,0:T(8,128)}, u32[]{:S(2)}) copy-start(f32[16,8,128]{2,1,0:T(8,128)} %get-tuple-element.18.rec) | copy-start | bytes 196612
  2.3 27.7 %all-to-all-start = ((f32[32,16,128]{2,1,0:T(8,128)}), f32[32,16,128]{2,1,0:T(8,128)S(1)}, u32[]{:S(2)}, u32[]{:S(2)}) async-start(f32[32,16,128]{2,1,0:T(8,128)} %get-tuple-element.22), calls=%async_computation | async-start | bytes 524288 | tf_op jit(solution)/shard_map/all_to_all | solution.py:548
  15.3 4.9 %collective-permute-start = (f32[1,8,128]{2,1,0:T(8,128)S(1)}, f32[1,8,128]{2,1,0:T(8,128)S(1)}, u32[]{:S(2)}, u32[]{:S(2)}) collective-permute-start(f32[1,8,128]{2,1,0:T(8,128)S(1)} %copy-done.11), channel_id=1, source_target_pairs={{0,32},{32,64},{64,96},{96,128},{128,160},{160,192},{192,224},{224... | collective-permute-start | bytes 12296 | tf_op jit(solution)/shard_map/ppermute | solution.py:544
  18.7 0.7 copy-start.9
  18.7 4.5 %collective-permute-start.1 = (f32[1,8,128]{2,1,0:T(8,128)S(1)}, f32[1,8,128]{2,1,0:T(8,128)S(1)}, u32[]{:S(2)}, u32[]{:S(2)}) collective-permute-start(f32[1,8,128]{2,1,0:T(8,128)S(1)} %copy-done.10), channel_id=1, source_target_pairs={{32,0},{64,32},{96,64},{128,96},{160,128},{192,160},{224,192},{256... | collective-permute-start | bytes 12296 | tf_op jit(solution)/shard_map/ppermute | solution.py:544
  19.4 0.7 copy-start.8
  20.1 3.2 %copy-start.2 = (f32[16,256]{1,0:T(8,128)S(1)}, f32[16,256]{1,0:T(8,128)}, u32[]{:S(2)}) copy-start(f32[16,256]{1,0:T(8,128)} %smoothing.5) | copy-start | bytes 49156
  20.2 3.0 %copy-start.7 = (s32[16]{0:T(128)S(1)}, s32[16]{0:T(128)}, u32[]{:S(2)}) copy-start(s32[16]{0:T(128)} %counts_ref.1) | copy-start | bytes 196
  23.3 6.8 %copy-start.4 = (f32[16,256]{1,0:T(8,128)S(1)}, f32[16,256]{1,0:T(8,128)}, u32[]{:S(2)}) copy-start(f32[16,256]{1,0:T(8,128)} %energy.1) | copy-start | bytes 49156
  30.0 0.7 copy-start.5
  30.0 0.7 copy-start.6
  44.2 20.4 %all-to-all-start.1 = ((f32[32,4,128]{2,1,0:T(4,128)}), f32[32,4,128]{2,1,0:T(4,128)S(1)}, u32[]{:S(2)}, u32[]{:S(2)}) async-start(f32[32,4,128]{2,1,0:T(4,128)} %get-tuple-element.29), calls=%async_computation.1 | async-start | bytes 131072 | tf_op jit(solution)/shard_map/all_to_all | solution.py:548
  53.9 1.2 %collective-permute-start.2 = (f32[1,2,128]{2,1,0:T(2,128)S(1)}, f32[1,2,128]{2,1,0:T(2,128)S(1)}, u32[]{:S(2)}, u32[]{:S(2)}) collective-permute-start(f32[1,2,128]{2,1,0:T(2,128)S(1)} %get-tuple-element.27), channel_id=1, source_target_pairs={{0,32},{32,64},{64,96},{96,128},{128,160},{160,192},{192,224},{224... | collective-permute-start | bytes 3080 | tf_op jit(solution)/shard_map/ppermute | solution.py:544
  53.9 4.5 %collective-permute-start.3 = (f32[1,2,128]{2,1,0:T(2,128)S(1)}, f32[1,2,128]{2,1,0:T(2,128)S(1)}, u32[]{:S(2)}, u32[]{:S(2)}) collective-permute-start(f32[1,2,128]{2,1,0:T(2,128)S(1)} %get-tuple-element.28), channel_id=1, source_target_pairs={{32,0},{64,32},{96,64},{128,96},{160,128},{192,160},{224,192},{256... | collective-permute-start | bytes 3080 | tf_op jit(solution)/shard_map/ppermute | solution.py:544
  58.4 6.2 %copy-start.1 = (f32[3,16,256]{2,1,0:T(8,128)S(1)}, f32[3,16,256]{2,1,0:T(8,128)}, u32[]{:S(2)}) copy-start(f32[3,16,256]{2,1,0:T(8,128)} %pos.3) | copy-start | bytes 147460
  58.4 6.2 %copy-start.3 = (f32[3,16,256]{2,1,0:T(8,128)S(1)}, f32[3,16,256]{2,1,0:T(8,128)}, u32[]{:S(2)}) copy-start(f32[3,16,256]{2,1,0:T(8,128)} %vel.1) | copy-start | bytes 147460

commit v5 on v4

--- a/solution.py
+++ b/solution.py
@@ -298,25 +298,51 @@
         return c + 1 if p == 0 else jnp.where(c < self.cells // 2, 0, self.cells + 1)
 
 
-def near_density_kernel(
-    counts_ref, rec, rim_lo, rim_hi, smoothing, sums, left, order, table, right, counts, copied, *scratch
-):
-    copy = pltpu.make_async_copy(counts_ref, counts, copied)
-    copy.start()
-    fill_table(table, rec, rim_lo, rim_hi, None, 8)
+class Indexed:
+    def __init__(self, function):
+        self.function = function
+
+    def __getitem__(self, place):
+        return self.function(*place)
+
+
+def operands_kernel(counts_ref, send_ref, rec, smoothing, left, right, order, counts, copied):
+    del send_ref
+    lists = begin((counts_ref, counts, copied.at[0]))
     fill_left(rec, smoothing, left)
 
     def step(t):
-        right[t] = right_operand(table[t], True)
-
-    for_cells(table.shape[0], step)
-    copy.wait()
+        right[t] = right_operand(rec[t], True)
+
+    for_cells(rec.shape[0], step)
+    finish_all(lists)
     sort_cells(counts, order)
+
+
+def near_density_kernel(order_ref, rec, rim_lo, rim_hi, left, own, sums, order, copied, table, right, *scratch):
+    lists = begin((order_ref, order, copied.at[0]))
+    cells = rec.shape[0]
+    for t, rim in enumerate((rim_lo, rim_hi)):
+        table[t] = rim[0]
+        right[t] = right_operand(rim[0], True)
+
+    def side(c):
+        return (c >= cells // 2).astype(jnp.int32)
 
     def store(c, row):
         sums[pl.ds(c, 1), :] = row
 
-    density_sums(order, near_partners(rec.shape[0]), [(0,), (1,)], table, right, left, *scratch, store)
+    finish_all(lists)
+    density_sums(
+        order,
+        Indexed(lambda p, c: (p, c)),
+        [(0,), (1,)],
+        Indexed(lambda at, *rest: table[(side(at[1]), *rest)] if at[0] else rec[(at[1], *rest)]),
+        Indexed(lambda p, c: right[side(c)] if p else own[c]),
+        left,
+        *scratch,
+        store,
+    )
 
 
 def density_kernel(
@@ -593,17 +619,25 @@
             pltpu.VMEM((P_SIZE, HALF), bf16),
         ]
 
-    near, left, order = call(
-        near_density_kernel,
+    left, own, order = call(
+        operands_kernel,
         [
-            shape(cells, P_SIZE),
             jax.ShapeDtypeStruct((cells, P_SIZE, HALF), bf16),
+            jax.ShapeDtypeStruct((cells, K_ROWS, P_SIZE), bf16),
             jax.ShapeDtypeStruct((cells,), jnp.int32),
         ],
         [],
-        [cell_counts],
-        [rec, rim_lo, rim_hi, smoothing],
-        tables(near_width) + [pltpu.SMEM((cells,), jnp.int32), pltpu.SemaphoreType.DMA] + sums(1),
+        [cell_counts, send],
+        [rec, smoothing],
+        [pltpu.SMEM((cells,), jnp.int32), pltpu.SemaphoreType.DMA((1,))],
+    )
+    (near,) = call(
+        near_density_kernel,
+        [shape(cells, P_SIZE)],
+        [],
+        [order],
+        [rec, rim_lo, rim_hi, left, own],
+        [pltpu.SMEM((cells,), jnp.int32), pltpu.SemaphoreType.DMA((1,))] + tables(2) + sums(1),
     )
     density, press, press_rec, first, last, press_out = call(
         density_kernel,

time: 98.3 us -> 97.9 us (level); the launches traced: 98.7 us -> 97.1 us
  Pallas kernels: 44.3 us -> 42.4 us
  waiting for transfers between devices: 7.02 us -> 5.34 us
  starting transfers between devices: 26.6 us -> 28.2 us
    pallas_call x6 -> x7, Pallas kernels: 44.3 us -> 42.4 us  [call(): pl.pallas_call(kernel, out_shape=tuple(outs), in_specs=[SMEM] * len(smem)...]
    ppermute x4, waiting for transfers between devices: 7.02 us -> 5.34 us  [to_neighbours(): return (lax.ppermute(last, axis, up), lax.ppermute(first, axis, down))]
    ppermute x4, starting transfers between devices: 3.88 us -> 5.15 us  [to_neighbours(): return (lax.ppermute(last, axis, up), lax.ppermute(first, axis, down))]
where the time goes in v5:
time: 97.9 us; the launch traced here: 97.1 us
  Pallas kernels  42.4 us (43%)
  starting transfers between devices  28.2 us (29%)
  blocking collectives  18.1 us (18%)
  waiting for transfers between devices  5.34 us (5%)
  local copies, waits for them, and re-layouts  2.11 us (2%)
    pallas_call x7, Pallas kernels, call(): pl.pallas_call(kernel, out_shape=tuple(outs), in_specs=[SMEM] * len(smem)...  42.4 us
    all_to_all x2, starting transfers between devices, exchange(): return lax.all_to_all(value, 'sub', split_axis=0, concat_axis=0, tiled=True)  23.1 us
    all_to_all x1, blocking collectives, exchange(): return lax.all_to_all(value, 'sub', split_axis=0, concat_axis=0, tiled=True)  18.1 us
    ppermute x4, waiting for transfers between devices, to_neighbours(): return (lax.ppermute(last, axis, up), lax.ppermute(first, axis, down))  5.34 us
    ppermute x4, starting transfers between devices, to_neighbours(): return (lax.ppermute(last, axis, up), lax.ppermute(first, axis, down))  5.15 us
  transfers between devices with their start and end apart: 6, of which 3 were waited for; matrix products, arithmetic and copies ran while one was open for 0% of the time, Pallas kernels for 13%

profile of v5, /device:TPU:25, one launch (start us, length us, event | category | flops | bytes accessed | tf_op | source)
XLA Modules:
  0.0 97.1 jit_solution(16677873709496273228)
XLA Ops:
  0.6 1.7 %shard_map.121 = (f32[16,8,128]{2,1,0:T(8,128)}, f32[1,8,128]{2,1,0:T(8,128)}, f32[1,8,128]{2,1,0:T(8,128)}, f32[32,16,128]{2,1,0:T(8,128)}) custom-call(s32[16]{0:T(128)} %counts_ref.1, s32[2,32]{1,0:T(2,128)} %bitcast.13, f32[3,16,256]{2,1,0:T(8,128)} %pos.3, f32[16,256]{1,0:T(8,128)} %mass.1), custom_call_target="tpu_custom_call" | custom-call | tf_op jit(solution)/shard_map/pallas_call | solution.py:554
  2.3 13.0 %all-to-all-start = ((f32[32,16,128]{2,1,0:T(8,128)}), f32[32,16,128]{2,1,0:T(8,128)S(1)}, u32[]{:S(2)}, u32[]{:S(2)}) async-start(f32[32,16,128]{2,1,0:T(8,128)} %get-tuple-element.22), calls=%async_computation | async-start | bytes 524288 | tf_op jit(solution)/shard_map/all_to_all | solution.py:574
  15.3 3.4 %collective-permute-start = (f32[1,8,128]{2,1,0:T(8,128)S(1)}, f32[1,8,128]{2,1,0:T(8,128)S(1)}, u32[]{:S(2)}, u32[]{:S(2)}) collective-permute-start(f32[1,8,128]{2,1,0:T(8,128)S(1)} %copy-done.11), channel_id=1, source_target_pairs={{0,32},{32,64},{64,96},{96,128},{128,160},{160,192},{192,224},{224... | collective-permute-start | bytes 12296 | tf_op jit(solution)/shard_map/ppermute | solution.py:570
  18.7 0.7 copy-done.9
  19.4 0.1 iota_compare_fusion
  19.4 0.1 lt.29
  19.5 0.5 copy-done.8
  20.1 0.1 copy.15
  20.1 0.1 squeeze.7
  20.2 0.0 copy-start.6
  20.3 0.5 copy-done.2
  20.8 0.1 copy-done.6
  20.9 1.5 %shard_map.122 = (bf16[16,256,128]{2,1,0:T(8,128)(2,1)S(1)}, bf16[16,32,256]{2,1,0:T(8,128)(2,1)S(1)}, s32[16]{0:T(128)S(1)}) custom-call(s32[16]{0:T(128)S(1)} %copy-done.7, s32[2,32]{1,0:T(2,128)S(1)} %bitcast.14, f32[16,8,128]{2,1,0:T(8,128)S(1)} %copy-done, f32[16,256]{1,0:T(8,128)S(1)} %copy-done.2), custom_call_target="tpu_custom_call" | custom-call | tf_op jit(solution)/shard_map/pallas_call | solution.py:554
  22.4 0.8 collective-permute-done.1.rim_hi
  23.3 5.6 %shard_map.123.near = f32[16,256]{1,0:T(8,128)S(1)} custom-call(s32[16]{0:T(128)S(1)} %get-tuple-element.19.order_ref, f32[16,8,128]{2,1,0:T(8,128)S(1)} %copy-done, f32[1,8,128]{2,1,0:T(8,128)S(1)} %collective-permute-done.rim_lo, f32[1,8,128]{2,1,0:T(8,128)S(1)} %collective-permute-done.1.rim_hi, bf16[16,256,128]{2,1,0:T(8,128)(2,1)S(1)} %get-tuple-element.23.left, ...), custom_call_target="tpu_custom_call" | custom-call | tf_op jit(solution)/shard_map/pallas_call | solution.py:554
  28.9 12.4 %shard_map.124 = (f32[16,256]{1,0:T(8,128)}, f32[16,256]{1,0:T(8,128)S(1)}, f32[16,2,128]{2,1,0:T(2,128)S(1)}, f32[1,2,128]{2,1,0:T(2,128)S(1)}, f32[1,2,128]{2,1,0:T(2,128)S(1)}, /*index=5*/f32[32,4,128]{2,1,0:T(4,128)}) custom-call(s32[16]{0:T(128)S(1)} %get-tuple-element.19.order_ref, s32[8,16]{1,0:T(8,128)S(1)} %bitcast.10, s32[2,32]{1,0:T(2,128)S(1)} %bitcast.15, ...), custom_call_target="tpu_custom_call" | custom-call | tf_op jit(solution)/shard_map/pallas_call | solution.py:554
  41.3 10.1 %all-to-all-start.1 = ((f32[32,4,128]{2,1,0:T(4,128)}), f32[32,4,128]{2,1,0:T(4,128)S(1)}, u32[]{:S(2)}, u32[]{:S(2)}) async-start(f32[32,4,128]{2,1,0:T(4,128)} %get-tuple-element.29), calls=%async_computation.1 | async-start | bytes 131072 | tf_op jit(solution)/shard_map/all_to_all | solution.py:574
  51.4 1.8 %collective-permute-start.2 = (f32[1,2,128]{2,1,0:T(2,128)S(1)}, f32[1,2,128]{2,1,0:T(2,128)S(1)}, u32[]{:S(2)}, u32[]{:S(2)}) collective-permute-start(f32[1,2,128]{2,1,0:T(2,128)S(1)} %get-tuple-element.27), channel_id=1, source_target_pairs={{0,32},{32,64},{64,96},{96,128},{128,160},{160,192},{192,224},{224... | collective-permute-start | bytes 3080 | tf_op jit(solution)/shard_map/ppermute | solution.py:570
  53.2 0.7 collective-permute-done.2.press_lo
  53.9 3.8 %collective-permute-done.3.press_hi = f32[1,2,128]{2,1,0:T(2,128)S(1)} collective-permute-done((f32[1,2,128]{2,1,0:T(2,128)S(1)}, f32[1,2,128]{2,1,0:T(2,128)S(1)}, u32[]{:S(2)}, u32[]{:S(2)}) %collective-permute-start.3) | collective-permute-done | bytes 1056 | tf_op jit(solution)/shard_map/ppermute | solution.py:570
  57.7 6.0 %shard_map.125.near = f32[16,8,256]{2,1,0:T(8,128)S(1)} custom-call(s32[16]{0:T(128)S(1)} %get-tuple-element.19.order_ref, f32[16,8,128]{2,1,0:T(8,128)S(1)} %copy-done, f32[1,8,128]{2,1,0:T(8,128)S(1)} %collective-permute-done.rim_lo, f32[1,8,128]{2,1,0:T(8,128)S(1)} %collective-permute-done.1.rim_hi, bf16[16,256,128]{2,1,0:T(8,128)(2,1)S(1)} %get-tuple-element.23.left, ...), custom_call_target="tpu_custom_call" | custom-call | tf_op jit(solution)/shard_map/pallas_call | solution.py:554
  63.7 14.2 %shard_map.126 = (f32[6,16,256]{2,1,0:T(8,128)}, f32[32,128]{1,0:T(8,128)S(1)}) custom-call(s32[16]{0:T(128)S(1)} %get-tuple-element.19.order_ref, s32[8,16]{1,0:T(8,128)S(1)} %bitcast.11, f32[16,8,128]{2,1,0:T(8,128)S(1)} %copy-done, f32[1,8,128]{2,1,0:T(8,128)S(1)} %collective-permute-done.rim_lo, f32[1,8,128]{2,1,0:T(8,128)S(1)} %collective-permute-done.1.rim_hi, ...), custom_call_target="tpu_custom_call" | custom-call | tf_op jit(solution)/shard_map/pallas_call | solution.py:554
  78.0 18.1 %all_to_all.15 = f32[32,1,128]{2,1,0:T(1,128)S(1)} all-to-all(f32[32,1,128]{2,1,0:T(1,128)S(1)} %bitcast.12), channel_id=1, replica_groups=mesh['slab'=16,'sub'=32] {'sub'}, dimensions={0} | all-to-all | bytes 32768 | tf_op jit(solution)/shard_map/all_to_all | solution.py:574
  96.1 1.0 %shard_map.127 = f32[6,256]{1,0:T(8,128)} custom-call(f32[32,128]{1,0:T(8,128)S(1)} %bitcast.9), custom_call_target="tpu_custom_call" | custom-call | tf_op jit(solution)/shard_map/pallas_call | solution.py:554
  (25 shorter events, 0.1 us)
Async XLA Ops:
  2.3 13.1 %copy-start.11 = (f32[1,8,128]{2,1,0:T(8,128)S(1)}, f32[1,8,128]{2,1,0:T(8,128)}, u32[]{:S(2)}) copy-start(f32[1,8,128]{2,1,0:T(8,128)} %get-tuple-element.20) | copy-start | bytes 12292
  2.3 16.4 %copy-start.10 = (f32[1,8,128]{2,1,0:T(8,128)S(1)}, f32[1,8,128]{2,1,0:T(8,128)}, u32[]{:S(2)}) copy-start(f32[1,8,128]{2,1,0:T(8,128)} %get-tuple-element.21) | copy-start | bytes 12292
  2.3 18.0 %copy-start = (f32[16,8,128]{2,1,0:T(8,128)S(1)}, f32[16,8,128]{2,1,0:T(8,128)}, u32[]{:S(2)}) copy-start(f32[16,8,128]{2,1,0:T(8,128)} %get-tuple-element.18.rec) | copy-start | bytes 196612
  2.3 26.6 %all-to-all-start = ((f32[32,16,128]{2,1,0:T(8,128)}), f32[32,16,128]{2,1,0:T(8,128)S(1)}, u32[]{:S(2)}, u32[]{:S(2)}) async-start(f32[32,16,128]{2,1,0:T(8,128)} %get-tuple-element.22), calls=%async_computation | async-start | bytes 524288 | tf_op jit(solution)/shard_map/all_to_all | solution.py:574
  15.3 7.1 %collective-permute-start = (f32[1,8,128]{2,1,0:T(8,128)S(1)}, f32[1,8,128]{2,1,0:T(8,128)S(1)}, u32[]{:S(2)}, u32[]{:S(2)}) collective-permute-start(f32[1,8,128]{2,1,0:T(8,128)S(1)} %copy-done.11), channel_id=1, source_target_pairs={{0,32},{32,64},{64,96},{96,128},{128,160},{160,192},{192,224},{224... | collective-permute-start | bytes 12296 | tf_op jit(solution)/shard_map/ppermute | solution.py:570
  18.7 0.7 copy-start.9
  18.7 4.5 %collective-permute-start.1 = (f32[1,8,128]{2,1,0:T(8,128)S(1)}, f32[1,8,128]{2,1,0:T(8,128)S(1)}, u32[]{:S(2)}, u32[]{:S(2)}) collective-permute-start(f32[1,8,128]{2,1,0:T(8,128)S(1)} %copy-done.10), channel_id=1, source_target_pairs={{32,0},{64,32},{96,64},{128,96},{160,128},{192,160},{224,192},{256... | collective-permute-start | bytes 12296 | tf_op jit(solution)/shard_map/ppermute | solution.py:570
  19.4 0.7 copy-start.8
  20.1 0.7 copy-start.2
  20.2 0.7 copy-start.6
  20.2 0.7 copy-start.7
  23.3 5.6 %copy-start.4 = (f32[16,256]{1,0:T(8,128)S(1)}, f32[16,256]{1,0:T(8,128)}, u32[]{:S(2)}) copy-start(f32[16,256]{1,0:T(8,128)} %energy.1) | copy-start | bytes 49156
  23.3 5.6 %copy-start.5 = (s32[16,8]{0,1:T(8,128)S(1)}, s32[16,8]{0,1:T(8,128)}, u32[]{:S(2)}) copy-start(s32[16,8]{0,1:T(8,128)} %param.17) | copy-start | bytes 1540
  41.3 22.4 %all-to-all-start.1 = ((f32[32,4,128]{2,1,0:T(4,128)}), f32[32,4,128]{2,1,0:T(4,128)S(1)}, u32[]{:S(2)}, u32[]{:S(2)}) async-start(f32[32,4,128]{2,1,0:T(4,128)} %get-tuple-element.29), calls=%async_computation.1 | async-start | bytes 131072 | tf_op jit(solution)/shard_map/all_to_all | solution.py:574
  51.4 2.5 %collective-permute-start.2 = (f32[1,2,128]{2,1,0:T(2,128)S(1)}, f32[1,2,128]{2,1,0:T(2,128)S(1)}, u32[]{:S(2)}, u32[]{:S(2)}) collective-permute-start(f32[1,2,128]{2,1,0:T(2,128)S(1)} %get-tuple-element.27), channel_id=1, source_target_pairs={{0,32},{32,64},{64,96},{96,128},{128,160},{160,192},{192,224},{224... | collective-permute-start | bytes 3080 | tf_op jit(solution)/shard_map/ppermute | solution.py:570
  53.2 4.5 %collective-permute-start.3 = (f32[1,2,128]{2,1,0:T(2,128)S(1)}, f32[1,2,128]{2,1,0:T(2,128)S(1)}, u32[]{:S(2)}, u32[]{:S(2)}) collective-permute-start(f32[1,2,128]{2,1,0:T(2,128)S(1)} %get-tuple-element.28), channel_id=1, source_target_pairs={{32,0},{64,32},{96,64},{128,96},{160,128},{192,160},{224,192},{256... | collective-permute-start | bytes 3080 | tf_op jit(solution)/shard_map/ppermute | solution.py:570
  57.7 6.0 %copy-start.1 = (f32[3,16,256]{2,1,0:T(8,128)S(1)}, f32[3,16,256]{2,1,0:T(8,128)}, u32[]{:S(2)}) copy-start(f32[3,16,256]{2,1,0:T(8,128)} %pos.3) | copy-start | bytes 147460
  57.7 6.0 %copy-start.3 = (f32[3,16,256]{2,1,0:T(8,128)S(1)}, f32[3,16,256]{2,1,0:T(8,128)}, u32[]{:S(2)}) copy-start(f32[3,16,256]{2,1,0:T(8,128)} %vel.1) | copy-start | bytes 147460
